TPU v7x, 256 devices: a whole 4x4x8 slice. The times are simulated.
256 devices in a mesh: frame: 64 (over x, y, z_lo), mp: 4 (over z_hi, core).
Axes of the slice: x: 4, y: 4, z: 8 (z_hi: 2, z_lo: 4; z = z_hi * 4 + z_lo), core: 2. Of those that a mesh axis runs over, the one named last changes fastest.
Arguments:
- kf_query: bfloat16 [4096, 4096], P('frame', 'mp'), may hold values from -6 to 6
- kf_kv: bfloat16 [2, 4096, 4096], P(None, 'frame', 'mp'), may hold values from -6 to 6
- cache_kv: bfloat16 [2, 16384, 4096], P(None, 'frame', 'mp'), may hold values from -6 to 6
- kf_latent: bfloat16 [4096, 4096], P('frame', 'mp'), may hold values from -6 to 6
- lift_weight: bfloat16 [4096, 8192], P('mp', 'frame'), may hold values from -0.09375 to 0.09375
- gap_latent: bfloat16 [256, 16, 16, 8192], P('frame', None, None, 'mp'), may hold values from -6 to 6
- query_map: bfloat16 [64, 128, 128], P('mp'), may hold values from -1 to 1
- key_map: bfloat16 [64, 128, 128], P('mp'), may hold values from -10 to 10
- frame_counts: int32 [256], P('frame'), may hold values from 1 to 16, as said below
- noise_step: int32 [1], replicated, may hold values from 200 to 800
Outputs:
- kf_out: bfloat16 [4096, 4096], P('frame', 'mp')
- gap_out: bfloat16 [256, 16, 16, 8192], P('frame', None, None, 'mp')
Inputs may be any that keep to these rules, and one draw needn't show every extreme that they name: `frame_counts`: some gap has 16 frames and some gap has 1.
All inputs are finite; a program needn't handle non-finite values.
Results may differ from a plain program's by a relative error of at most 0.0044.
Values may be sent and summed in bfloat16 or wider, within the bound.
No kernel may reach another device: no remote copies, remote signals or barrier semaphores. Data moves between devices by JAX's collectives and lax.ppermute only.
A program may use at most 128 MiB of HBM per device.

v0:
```python
import math

import jax
import jax.numpy as jnp
from jax import lax
from jax.sharding import PartitionSpec as P

HD = 128
STRIDE = 200


def extended(x, sides, width):
    for axis, dim in sides:
        size, length = (lax.axis_size(axis), x.shape[dim])
        up = [(i, (i + 1) % size) for i in range(size - 1)]
        down = [(j, i) for i, j in up]
        last = lax.slice_in_dim(x, length - width, length, axis=dim)
        initial = lax.slice_in_dim(x, 0, width, axis=dim)
        before = lax.ppermute(last, axis, up)
        after = lax.ppermute(initial, axis, down)
        x = jnp.concatenate([before, x, after], axis=dim)
    return x


def shifted(value, axis, steps):
    count = lax.axis_size(axis)
    initial, last = (max(0, -steps), min(count, count - steps))
    return lax.ppermute(value, axis, [(source, source + steps) for source in range(initial, last)])


def attend(queries, key_rows, value_rows, usable, heads):
    count_q = queries.shape[0]
    count_k = key_rows.shape[0]
    query_h = queries.reshape(count_q, heads, HD)
    key_h = key_rows.reshape(count_k, heads, HD)
    value_h = value_rows.reshape(count_k, heads, HD)
    scores = jnp.einsum(
        "qhd,khd->hqk", query_h, key_h, preferred_element_type=jnp.float32
    ) * HD ** (-0.5)
    scores = jnp.where(usable[None], scores, -1e30)
    highest = jnp.max(scores, axis=2, keepdims=True)
    probs = jnp.exp(scores - highest)
    totals = jnp.sum(probs, axis=2)
    weights = probs.astype(jnp.bfloat16)
    mixed = jnp.einsum("hqk,khd->qhd", weights, value_h, preferred_element_type=jnp.float32)
    return (mixed / jnp.transpose(totals)[:, :, None]).reshape(count_q, heads * HD)


def head_map(rows, maps):
    count = rows.shape[0]
    heads = maps.shape[0]
    split = rows.reshape(count, heads, HD)
    mapped = jnp.einsum("nhd,hde->nhe", split, maps, preferred_element_type=jnp.float32)
    return mapped.reshape(count, heads * HD).astype(jnp.bfloat16)


def signal_level(step):
    return jnp.cos((step / 1000.0 + 0.008) / 1.008 * (math.pi / 2)) ** 2


def denoise(
    latent, left, right, left_key, right_key, count, query_map, key_map, level_now, level_prev
):
    frames = latent.shape[0]
    tokf = latent.shape[1]
    width = latent.shape[2]
    heads = query_map.shape[0]
    index = jnp.arange(frames, dtype=jnp.int32)
    along = ((index + 1).astype(jnp.float32) / (count + 1).astype(jnp.float32))[:, None, None]
    noisy = latent.astype(jnp.float32)
    inputs = (
        noisy
        + (1.0 - along) * left.astype(jnp.float32)[None]
        + along * right.astype(jnp.float32)[None]
    ).astype(jnp.bfloat16)
    tokens = inputs.reshape(frames * tokf, width)
    queries = head_map(tokens, query_map)
    key_rows = jnp.concatenate([head_map(tokens, key_map), left_key, right_key], 0)
    value_rows = jnp.concatenate([tokens, left, right], 0)
    live = index < count
    usable = jnp.concatenate([jnp.repeat(live, tokf), jnp.ones((2 * tokf,), bool)])[None]
    guess = attend(queries, key_rows, value_rows, usable, heads).reshape(frames, tokf, width)
    clean = (noisy - jnp.sqrt(1.0 - level_now) * guess) / jnp.sqrt(level_now)
    stepped = jnp.sqrt(level_prev) * clean + jnp.sqrt(1.0 - level_prev) * guess
    return jnp.where(live[:, None, None], stepped, 0.0).astype(jnp.bfloat16)


def on_device(
    kf_query,
    kf_kv,
    cache_kv,
    kf_latent,
    lift_weight,
    gap_latent,
    query_map,
    key_map,
    frame_counts,
    noise_step,
):
    context = cache_kv.shape[1]
    block_rows = kf_query.shape[0]
    nearby = extended(cache_kv, (("frame", 1),), context)
    device_at = lax.axis_index("frame")
    places = device_at * context - context + jnp.arange(3 * context, dtype=jnp.int32)
    inside = (places >= 0) & (places < context * lax.axis_size("frame"))
    usable = jnp.concatenate([inside, jnp.ones((block_rows,), bool)])[None]
    key_rows = jnp.concatenate([nearby[0], kf_kv[0]], 0)
    value_rows = jnp.concatenate([nearby[1], kf_kv[1]], 0)
    key_heads = kf_query.shape[1] // HD
    updated = (
        kf_latent.astype(jnp.float32) + attend(kf_query, key_rows, value_rows, usable, key_heads)
    ).astype(jnp.bfloat16)
    partial_sums = jnp.dot(
        updated,
        lax.all_gather(lift_weight, "frame", axis=1, tiled=True),
        preferred_element_type=jnp.float32,
    )
    lifted = lax.psum_scatter(partial_sums, "mp", scatter_dimension=1, tiled=True).astype(
        jnp.bfloat16
    )
    lifted_keys = head_map(lifted, key_map)
    kf_local = frame_counts.shape[0]
    tokf = block_rows // kf_local
    width = lifted.shape[1]
    lifted_k = lifted.reshape(kf_local, tokf, width)
    keys_k = lifted_keys.reshape(kf_local, tokf, width)
    following = shifted(jnp.stack([lifted_k[0], keys_k[0]]), "frame", -1)
    right_all = jnp.concatenate([lifted_k[1:], following[0][None]], 0)
    right_keys = jnp.concatenate([keys_k[1:], following[1][None]], 0)
    step = noise_step[0].astype(jnp.float32)
    level_now = signal_level(step)
    level_prev = signal_level(step - STRIDE)

    def one_gap(latent, left, right, left_key, right_key, count):
        return denoise(
            latent,
            left,
            right,
            left_key,
            right_key,
            count,
            query_map,
            key_map,
            level_now,
            level_prev,
        )

    gap_out = jax.vmap(one_gap)(gap_latent, lifted_k, right_all, keys_k, right_keys, frame_counts)
    return (updated, gap_out)


def solution(mesh):
    placed = (
        P("frame", "mp"),
        P(None, "frame", "mp"),
        P(None, "frame", "mp"),
        P("frame", "mp"),
        P("mp", "frame"),
        P("frame", None, None, "mp"),
        P("mp", None, None),
        P("mp", None, None),
        P("frame"),
        P(),
    )
    return jax.shard_map(
        on_device,
        mesh=mesh,
        in_specs=placed,
        out_specs=(P("frame", "mp"), P("frame", None, None, "mp")),
        check_vma=False,
    )
```

profile of v0, /device:TPU:2, one launch (start us, length us, event | category | flops | bytes accessed | tf_op | source)
XLA Modules:
  0.0 676.5 jit_solution(12277476147658467825)
XLA Ops:
  8.0 1.5 copy.23
  9.4 9.0 %collective-permute-start.1 = (bf16[2,256,1024]{1,2,0:T(8,128)(2,1)S(1)}, bf16[2,256,1024]{1,2,0:T(8,128)(2,1)S(1)}, u32[]{:S(2)}, u32[]{:S(2)}) collective-permute-start(bf16[2,256,1024]{1,2,0:T(8,128)(2,1)S(1)} %copy.23), channel_id=1, source_target_pairs={{4,0},{8,4},{12,8},{16,12},{20,16},{24,20},{28,24},{32,28},{36,32}... | collective-permute-start | bytes 3145736 | tf_op jit(solution)/shard_map/ppermute | solution.py:20
  18.4 1.9 collective-permute-start
  21.5 31.7 %collective-permute-done.1 = bf16[2,256,1024]{1,2,0:T(8,128)(2,1)S(1)} collective-permute-done((bf16[2,256,1024]{1,2,0:T(8,128)(2,1)S(1)}, bf16[2,256,1024]{1,2,0:T(8,128)(2,1)S(1)}, u32[]{:S(2)}, u32[]{:S(2)}) %collective-permute-start.1) | collective-permute-done | bytes 1048608 | tf_op jit(solution)/shard_map/ppermute | solution.py:20
  53.2 34.4 %collective-permute-done = bf16[2,256,1024]{1,2,0:T(8,128)(2,1)} collective-permute-done((bf16[2,256,1024]{1,2,0:T(8,128)(2,1)S(1)}, bf16[2,256,1024]{1,2,0:T(8,128)(2,1)}, u32[]{:S(2)}, u32[]{:S(2)}) %collective-permute-start) | collective-permute-done | bytes 1048608 | tf_op jit(solution)/shard_map/ppermute | solution.py:19
  90.2 2.6 copy.28
  92.9 1.6 copy.26
  94.4 2.3 bitcast_reduce_fusion
  98.0 384.1 %all-gather.2.cloned.1.call-done = bf16[1024,8192]{1,0:T(8,128)(2,1)} async-done(((bf16[1024,128]{1,0:T(8,128)(2,1)}), bf16[1024,8192]{1,0:T(8,128)(2,1)}) %all-gather.2.cloned.1.call-update) | async-done | bytes 16777232 | tf_op jit(solution)/shard_map/all_gather | solution.py:115
  482.2 10.1 %fusion.91 = f32[64,8192]{1,0:T(8,128)} fusion(bf16[64,1024]{1,0:T(8,128)(2,1)S(1)} %fusion.67, bf16[1024,8192]{1,0:T(8,128)(2,1)} %all-gather.2.cloned.1.call-done), kind=kOutput, calls=%fused_computation.102 | convolution fusion | flops 1073741824 | bytes 19005440 | tf_op jit(solution)/shard_map/dot_general | solution.py:113
  493.6 64.3 %reduce-scatter.2.cloned.1.call-done = f32[64,2048]{1,0:T(8,128)} async-done(((f32[64,8192]{1,0:T(8,128)}), f32[64,2048]{1,0:T(8,128)}) %reduce-scatter.2.cloned.1.call-update) | async-done | bytes 524304 | tf_op jit(solution)/shard_map/reduce_scatter | solution.py:118
  561.6 5.0 collective-permute-start.2
  566.9 2.1 collective-permute-done.2
  569.1 3.8 fusion.10
  574.3 3.4 convert_bitcast_fusion
  577.7 3.0 copy.36
  580.7 12.5 %fusion = (f32[4,16,256]{2,1,0:T(8,128)S(1)}, f32[4,16,256,288]{2,3,1,0:T(8,128)}) fusion(pred[4,288]{1,0:T(4,128)(4,1)S(1)} %concatenate.77, bf16[1,16,16,128]{3,1,2,0:T(8,128)(2,1)S(1)} %get-tuple-element.19, bf16[4,256,16,128]{3,1,2,0:T(8,128)(2,1)} %convert_bitcast_fusion, bf16[16,128,128]{2,1,0:T(8,128)(2,1)S(1)} %copy-done, ...), kind=kOutput, calls=%fused_computation.2 | convolution fusion | flops 1779941376 | bytes 28378240 | tf_op jit(solution)/shard_map/vmap(qhd,khd->hqk)/dot_general | solution.py:37
  593.2 11.7 %fusion.1 = f32[4,16,256]{2,1,0:T(8,128)S(1)} fusion(f32[4,16,256,288]{2,3,1,0:T(8,128)} %get-tuple-element.18, f32[4,16,256]{2,1,0:T(8,128)S(1)} %get-tuple-element.17, pred[4,288]{1,0:T(4,128)(4,1)S(1)} %concatenate.77), kind=kLoop, calls=%fused_computation.3 | loop fusion | flops 18857984 | bytes 19006592 | tf_op jit(solution)/shard_map/vmap()/reduce_sum | solution.py:43
  604.9 15.2 %broadcast_multiply_fusion.1 = (f32[4,256,16,128]{1,3,2,0:T(8,128)}, f32[4,256,16,128]{1,3,2,0:T(8,128)}) fusion(f32[]{:T(128)} %bitcast.6, f32[]{:T(128)} %bitcast.20, f32[4,256,16]{1,2,0:T(8,128)S(1)} %bitcast.125, f32[4,16,256,288]{2,3,1,0:T(8,128)} %get-tuple-element.18, f32[4,16,256]{2,1,0:T(8,128)S(1)} %get-tuple-element.17, ...), kind=kOutput, calls=%fused_computation.39 | convolution fusion | flops 1251999744 | bytes 40502408 | tf_op jit(solution)/shard_map/vmap(hqk,khd->qhd)/dot_general | solution.py:45
  620.2 10.2 %copy.41 = f32[4,256,16,128]{3,2,1,0:T(8,128)} copy(f32[4,256,16,128]{1,3,2,0:T(8,128)} %get-tuple-element.2) | data formatting | bytes 16777216 | tf_op jit(solution)/shard_map/vmap()/mul | solution.py:83
  630.4 9.3 %mul.92 = f32[4,16,16,2048]{3,2,1,0:T(8,128)} reshape(f32[4,256,16,128]{3,2,1,0:T(8,128)} %copy.41) | data formatting | bytes 16777216 | tf_op jit(solution)/shard_map/vmap()/mul | solution.py:83
  639.7 10.3 %copy.42 = f32[4,256,16,128]{3,2,1,0:T(8,128)} copy(f32[4,256,16,128]{1,3,2,0:T(8,128)} %get-tuple-element.3) | data formatting | bytes 16777216 | tf_op jit(solution)/shard_map/vmap()/mul | solution.py:84
  649.9 9.3 %mul.96 = f32[4,16,16,2048]{3,2,1,0:T(8,128)} reshape(f32[4,256,16,128]{3,2,1,0:T(8,128)} %copy.42) | data formatting | bytes 16777216 | tf_op jit(solution)/shard_map/vmap()/mul | solution.py:84
  659.2 10.5 %fusion.15 = bf16[4,16,16,2048]{3,2,1,0:T(8,128)(2,1)} fusion(f32[4,16,16,2048]{3,2,1,0:T(8,128)} %mul.96, f32[4,16,16,2048]{3,2,1,0:T(8,128)} %mul.92, bf16[4,16,16,2048]{3,2,1,0:T(8,128)(2,1)} %param.15, f32[]{:T(128)} %bitcast.19, f32[]{:T(128)} %bitcast.5, pred[4,16]{1,0:T(4,128)(4,1)S(1)} %iota_compare_fusion), kind=kLoop, calls=%fused_computation.19 | loop fusion | flops 14680064 | bytes 25165896 | tf_op jit(solution)/shard_map/vmap()/convert_element_type | solution.py:85
  (60 shorter events, 11.5 us)
Async XLA Ops:
  7.2 573.6 %copy-start = (bf16[16,128,128]{2,1,0:T(8,128)(2,1)S(1)}, bf16[16,128,128]{2,1,0:T(8,128)(2,1)}, u32[]{:S(2)}) copy-start(bf16[16,128,128]{2,1,0:T(8,128)(2,1)} %param.16) | copy-start | bytes 1572868
  7.2 475.0 %all-gather.2.cloned.1.call-start = ((), (), s32[]{:S(2)}) async-start(), calls=%async_computation.1 | async-start | bytes 17039360 | tf_op jit(solution)/shard_map/all_gather | solution.py:115
  7.9 550.0 %reduce-scatter.2.cloned.1.call-start = ((), (), s32[]{:S(2)}) async-start(), calls=%async_computation.2 | async-start | bytes 2621440 | tf_op jit(solution)/shard_map/reduce_scatter | solution.py:118
  9.4 43.7 %collective-permute-start.1 = (bf16[2,256,1024]{1,2,0:T(8,128)(2,1)S(1)}, bf16[2,256,1024]{1,2,0:T(8,128)(2,1)S(1)}, u32[]{:S(2)}, u32[]{:S(2)}) collective-permute-start(bf16[2,256,1024]{1,2,0:T(8,128)(2,1)S(1)} %copy.23), channel_id=1, source_target_pairs={{4,0},{8,4},{12,8},{16,12},{20,16},{24,20},{28,24},{32,28},{36,32}... | collective-permute-start | bytes 3145736 | tf_op jit(solution)/shard_map/ppermute | solution.py:20
  18.4 69.1 %collective-permute-start = (bf16[2,256,1024]{1,2,0:T(8,128)(2,1)S(1)}, bf16[2,256,1024]{1,2,0:T(8,128)(2,1)}, u32[]{:S(2)}, u32[]{:S(2)}) collective-permute-start(bf16[2,256,1024]{1,2,0:T(8,128)(2,1)S(1)} %copy.23), channel_id=1, source_target_pairs={{0,4},{4,8},{8,12},{12,16},{16,20},{20,24},{24,28},{28,32},{32,36}... | collective-permute-start | bytes 3145736 | tf_op jit(solution)/shard_map/ppermute | solution.py:19
  90.2 4.2 copy-start.7
  94.4 2.8 copy-start.4
  96.7 1.2 copy-start.6
  98.0 394.3 %copy-start.5 = (bf16[64,1024]{1,0:T(8,128)(2,1)}, bf16[64,1024]{1,0:T(8,128)(2,1)S(1)}, u32[]{:S(2)}) copy-start(bf16[64,1024]{1,0:T(8,128)(2,1)S(1)} %fusion.67) | copy-start | bytes 393220
  98.0 395.3 %copy-start.8 = (s32[4]{0:T(128)S(1)}, s32[4]{0:T(128)}, u32[]{:S(2)}) copy-start(s32[4]{0:T(128)} %param.18) | copy-start | bytes 52
  98.0 459.9 %copy-start.3 = (bf16[16,128,128]{2,1,0:T(8,128)(2,1)S(1)}, bf16[16,128,128]{2,1,0:T(8,128)(2,1)}, u32[]{:S(2)}) copy-start(bf16[16,128,128]{2,1,0:T(8,128)(2,1)} %param.17) | copy-start | bytes 1572868
  561.6 7.3 %collective-permute-start.2 = (bf16[2,16,2048]{2,1,0:T(8,128)(2,1)S(1)}, bf16[2,16,2048]{2,1,0:T(8,128)(2,1)S(1)}, u32[]{:S(2)}, u32[]{:S(2)}) collective-permute-start(bf16[2,16,2048]{2,1,0:T(8,128)(2,1)S(1)} %pad_maximum_fusion.1), channel_id=1, source_target_pairs={{4,0},{8,4},{12,8},{16,12},{20,16},{24,20},{28,24},{32,28},{36,32}... | collective-permute-start | bytes 393224 | tf_op jit(solution)/shard_map/ppermute | solution.py:28
  574.3 6.4 copy-start.2
  659.2 10.5 %copy-start.1 = (bf16[16,128,128]{2,1,0:T(8,128)(2,1)S(1)}, bf16[16,128,128]{2,1,0:T(8,128)(2,1)}, u32[]{:S(2)}) copy-start(bf16[16,128,128]{2,1,0:T(8,128)(2,1)} %param.16) | copy-start | bytes 1572868
Sparse Core Ops, SparseCore 0:
  9.7 472.3 all-gather.1
  492.4 65.4 reduce-scatter.1
where the time goes:
time: 678 us; the launch traced here: 677 us
  waiting for transfers between devices  517 us (76%)
  local copies, waits for them, and re-layouts  52.2 us (8%)
  matrix products  45.5 us (7%)
  other arithmetic  30.2 us (4%)
  starting transfers between devices  16 us (2%)
  between operations  15.4 us (2%)
    all_gather x1, waiting for transfers between devices, on_device(): lax.all_gather(lift_weight, 'frame', axis=1, tiled=True)  384 us
    reduce_scatter x1, waiting for transfers between devices, on_device(): lax.psum_scatter(partial_sums, 'mp', scatter_dimension=1, tiled=True)  64.3 us
    ppermute x1, waiting for transfers between devices, extended(): before = lax.ppermute(last, axis, up)  34.4 us
    ppermute x1, waiting for transfers between devices, extended(): after = lax.ppermute(initial, axis, down)  31.7 us
    mul x2, local copies, waits for them, and re-layouts, denoise(): stepped = jnp.sqrt(level_prev) * clean + jnp.sqrt(1.0 - level_prev) * guess  19.5 us
    mul x2, local copies, waits for them, and re-layouts, denoise(): clean = (noisy - jnp.sqrt(1.0 - level_now) * guess) / jnp.sqrt(level_now)  19.5 us
    dot_general x2, matrix products, attend(): jnp.einsum('hqk,khd->qhd', weights, value_h, preferred_element_type=jnp.f...  15.9 us
    dot_general x2, matrix products, attend(): jnp.einsum('qhd,khd->hqk', query_h, key_h, preferred_element_type=jnp.flo...  14.7 us
  transfers between devices with their start and end apart: 5, of which 5 were waited for; matrix products, arithmetic and copies ran while one was open for 2% of the time, Pallas kernels for 0%

commit v1 on v0

v1 whole, which is shorter than its diff:
```python
import functools
import math

import jax
import jax.numpy as jnp
from jax import lax
from jax.experimental import pallas as pl
from jax.experimental.pallas import tpu as pltpu
from jax.sharding import Mesh
from jax.sharding import PartitionSpec as P

HD = 128
STRIDE = 200
NEG = -1e30
BF = jnp.bfloat16
F32 = jnp.float32
SCALE = HD ** (-0.5)
SIZES = (4, 4, 4, 2, 2)
AXES = ("x", "y", "z", "h", "c")
FRAME = ("x", "y", "z")
N_FRAME = 64


def nt(a, b):
    return lax.dot_general(a, b, (((1,), (1,)), ((), ())), preferred_element_type=F32)


def nn(a, b):
    return jnp.dot(a, b, preferred_element_type=F32)


def kf_kernel(edge, q, kv, own, prev, nxt, latent, out):
    has_prev = edge[0] > 0
    has_next = edge[1] > 0
    for h in range(q.shape[1] // HD):
        cols = slice(h * HD, (h + 1) * HD)
        query = q[:, cols]
        scores = [
            jnp.where(has_prev, nt(query, prev[0, :, cols]) * SCALE, NEG),
            nt(query, own[0, :, cols]) * SCALE,
            jnp.where(has_next, nt(query, nxt[0, :, cols]) * SCALE, NEG),
            nt(query, kv[0, :, cols]) * SCALE,
        ]
        top = functools.reduce(jnp.maximum, [jnp.max(s, axis=1, keepdims=True) for s in scores])
        probs = [jnp.exp(s - top) for s in scores]
        total = sum(jnp.sum(p, axis=1, keepdims=True) for p in probs)
        mixed = sum(
            nn(p.astype(BF), v[1, :, cols]) for p, v in zip(probs, (prev, own, nxt, kv))
        )
        out[:, cols] = (latent[:, cols].astype(F32) + mixed / total).astype(BF)


def kf_attention(edge, q, kv, own, prev, nxt, latent):
    rows, width = q.shape
    ctx = own.shape[1]
    step = 2 * HD
    flat = pl.BlockSpec((rows, step), lambda i, e: (0, i))
    pair = pl.BlockSpec((2, rows, step), lambda i, e: (0, 0, i))
    wide = pl.BlockSpec((2, ctx, step), lambda i, e: (0, 0, i))
    return pl.pallas_call(
        kf_kernel,
        grid_spec=pltpu.PrefetchScalarGridSpec(
            num_scalar_prefetch=1,
            grid=(width // step,),
            in_specs=[flat, pair, wide, wide, wide, flat],
            out_specs=flat,
        ),
        out_shape=jax.ShapeDtypeStruct((rows, width), BF),
        cost_estimate=pl.CostEstimate(
            flops=4 * rows * width * (3 * ctx + rows),
            bytes_accessed=2 * (12 * ctx * width + 8 * rows * width) // 2,
            transcendentals=rows * (width // HD) * (3 * ctx + rows),
        ),
        name="kf_attention",
    )(edge, q, kv, own, prev, nxt, latent)


def lift_kernel(info, *refs):
    acts = refs[0:8]
    weights = refs[8:12]
    out = refs[12]
    rows, total = refs[13:]
    z = info[0]

    @pl.when(pl.program_id(0) == 0)
    def _():
        for s in range(2):
            for d in range(4):
                rows[s, d * 64 : (d + 1) * 64, :] = acts[s * 4 + d][...]

    total[...] = jnp.zeros_like(total)
    for d in range(4):
        total[info[5 + d]] += nn(rows[info[1 + d]], weights[d][0])
    for d in range(4):
        to = lax.rem(z + 4 - d, 4)
        for h in range(2):
            out[to * 2 + h] = total[h, d * 64 : (d + 1) * 64, :].astype(BF)


def lift(info, acts, weights):
    rows, width = acts[0].shape
    whole = pl.BlockSpec((rows, width), lambda i, e: (0, 0))
    tile = pl.BlockSpec((1, width, HD), lambda i, e: (i, 0, 0))
    return pl.pallas_call(
        lift_kernel,
        grid_spec=pltpu.PrefetchScalarGridSpec(
            num_scalar_prefetch=1,
            grid=(4,),
            in_specs=[whole] * 8 + [tile] * 4,
            out_specs=pl.BlockSpec((8, rows, HD), lambda i, e: (0, 0, i)),
            scratch_shapes=[
                pltpu.VMEM((2, 4 * rows, width), BF),
                pltpu.VMEM((2, 4 * rows, HD), F32),
            ],
        ),
        out_shape=jax.ShapeDtypeStruct((8, rows, 4 * HD), BF),
        cost_estimate=pl.CostEstimate(
            flops=2 * 4 * rows * 2 * width * 8 * HD,
            bytes_accessed=2 * (16 * width * HD + 8 * rows * width + 32 * rows * HD),
            transcendentals=0,
        ),
        name="lift",
    )(info, *acts, *weights)


def combine_kernel(parts, out, first):
    for z in range(4):
        for y in range(4):
            cols = slice(y * HD, (y + 1) * HD)
            place = slice((y * 4 + z) * HD, (y * 4 + z + 1) * HD)
            total = parts[2 * z, :, cols].astype(F32) + parts[2 * z + 1, :, cols].astype(F32)
            total = total.astype(BF)
            out[:, place] = total
            first[:, place] = total[: first.shape[0]]


def combine(parts, tokf):
    rows = parts.shape[1]
    width = 4 * parts.shape[2]
    return pl.pallas_call(
        combine_kernel,
        out_shape=(
            jax.ShapeDtypeStruct((rows, width), BF),
            jax.ShapeDtypeStruct((tokf, width), BF),
        ),
        cost_estimate=pl.CostEstimate(
            flops=2 * rows * width, bytes_accessed=6 * rows * width, transcendentals=0
        ),
        name="combine",
    )(parts)


def gap_kernel(first, heads, count, along, keep, move, latent, left, right, qmap, kmap, *rest):
    out = rest[-1]
    gap = first + pl.program_id(0)
    frames, tokf = latent.shape[1], latent.shape[2]
    toks = frames * tokf
    live = count[gap] * tokf
    keys = lax.broadcasted_iota(jnp.int32, (1, toks), 1)
    bias = jnp.where(keys < live, 0.0, NEG).astype(F32)
    ones_a = jnp.ones((toks, HD), BF)
    ones_b = jnp.ones((2 * tokf, HD), BF)
    for h in range(heads):
        cols = slice(h * HD, (h + 1) * HD)
        lo, hi = left[:, cols], right[:, cols]
        lo32, hi32 = lo.astype(F32), hi.astype(F32)
        tokens = jnp.concatenate(
            [
                (
                    latent[0, j, :, cols].astype(F32)
                    + (1.0 - along[gap, j]) * lo32
                    + along[gap, j] * hi32
                ).astype(BF)
                for j in range(frames)
            ],
            axis=0,
        )
        sides = jnp.concatenate([lo, hi], axis=0)
        mapped = nn(tokens, jnp.concatenate([qmap[h], kmap[h]], axis=1)).astype(BF)
        query, key = mapped[:, :HD], mapped[:, HD:]
        side_key = nn(sides, kmap[h]).astype(BF)
        sa = nt(query, key) + bias
        sb = nt(query, side_key)
        top = jnp.maximum(
            jnp.max(sa, axis=1, keepdims=True), jnp.max(sb, axis=1, keepdims=True)
        )
        pa = jnp.exp((sa - top) * SCALE).astype(BF)
        pb = jnp.exp((sb - top) * SCALE).astype(BF)
        mixed = nn(pa, jnp.concatenate([tokens, ones_a], axis=1)) + nn(
            pb, jnp.concatenate([sides, ones_b], axis=1)
        )
        guess = mixed[:, :HD] / mixed[:, HD:]
        for j in range(frames):
            rows = slice(j * tokf, (j + 1) * tokf)
            out[0, j, :, cols] = (
                latent[0, j, :, cols].astype(F32) * keep[gap, j] + guess[rows] * move[gap, j]
            ).astype(BF)


def denoise(first, gaps, tables, latent, left, right, qmap, kmap, heads=4, into=None):
    _, frames, tokf, width = latent.shape
    step = heads * HD
    spot = pl.BlockSpec((1, frames, tokf, step), lambda g, i, *s: (first + g, 0, 0, i))
    side = pl.BlockSpec((tokf, step), lambda g, i, *s: (g, i))
    maps = pl.BlockSpec((heads, HD, HD), lambda g, i, *s: (i, 0, 0))
    extra = [] if into is None else [into]
    specs = [spot, side, side, maps, maps] + [pl.BlockSpec(memory_space=pl.ANY)] * len(extra)
    toks = frames * tokf
    return pl.pallas_call(
        functools.partial(gap_kernel, first, heads),
        grid_spec=pltpu.PrefetchScalarGridSpec(
            num_scalar_prefetch=4,
            grid=(gaps, width // step),
            in_specs=specs,
            out_specs=spot,
        ),
        out_shape=jax.ShapeDtypeStruct(latent.shape, BF),
        input_output_aliases={9: 0} if extra else {},
        cost_estimate=pl.CostEstimate(
            flops=gaps * 2 * toks * width * (2 * HD + 2 * (toks + 2 * tokf)),
            bytes_accessed=4 * gaps * toks * width,
            transcendentals=gaps * (width // HD) * toks * (toks + 2 * tokf),
        ),
        name=f"denoise_{first}",
    )(*tables, latent, left, right, qmap, kmap, *extra)


def signal_level(step):
    return jnp.cos((step / 1000.0 + 0.008) / 1.008 * (math.pi / 2)) ** 2


def ring(size, by):
    return [(i, (i + by) % size) for i in range(size)]


def gather_weight(weight):
    pieces = [weight] + [lax.ppermute(weight, "y", ring(4, d)) for d in (1, 2, 3)]
    y = lax.axis_index("y")
    table = jnp.stack(pieces)
    table = jnp.take(table, (y - jnp.arange(4)) % 4, axis=0)
    moved = []
    for d in range(4):
        perm = [(a * 2 + b, ((a + d + b) % 4) * 2 + (a & 1)) for a in range(4) for b in range(2)]
        moved.append(lax.ppermute(table, ("x", "c"), perm))
    return moved


def on_device(
    kf_query,
    kf_kv,
    cache_kv,
    kf_latent,
    lift_weight,
    gap_latent,
    query_map,
    key_map,
    frame_counts,
    noise_step,
):
    x, y, z, h, c = (lax.axis_index(a) for a in AXES)
    frame = (x * 4 + y) * 4 + z
    up = [(i, i + 1) for i in range(N_FRAME - 1)]
    down = [(j, i) for i, j in up]
    prev = lax.ppermute(cache_kv, FRAME, up)
    nxt = lax.ppermute(cache_kv, FRAME, down)
    weights = gather_weight(lift_weight)

    edge = jnp.stack([frame > 0, frame < N_FRAME - 1]).astype(jnp.int32)
    updated = kf_attention(edge, kf_query, kf_kv, cache_kv, prev, nxt, kf_latent)

    mine = [updated] + [lax.ppermute(updated, "z", ring(4, d)) for d in (1, 2, 3)]
    theirs = [lax.ppermute(a, "c", ring(2, 1)) for a in mine]

    core = [(x - d - c) % 2 for d in range(4)]
    at = [(x - d - s) % 4 for d, s in zip(range(4), core)]
    info = jnp.stack(
        [z] + [(s != c).astype(jnp.int32) for s in core] + [a // 2 for a in at]
    ).astype(jnp.int32)
    parts = lift(info, mine + theirs, weights)
    parts = lax.all_to_all(parts, ("z", "h"), 0, 0, tiled=False)

    gaps, frames, tokf, width = gap_latent.shape
    lifted, initial = combine(parts, tokf)
    following = lax.ppermute(initial, FRAME, down)

    step = noise_step[0].astype(F32)
    now = signal_level(step)
    before = signal_level(step - STRIDE)
    slots = jnp.arange(frames, dtype=jnp.int32)[None]
    counts = frame_counts[:, None]
    along = (slots + 1).astype(F32) / (counts + 1).astype(F32)
    live = slots < counts
    keep = jnp.where(live, jnp.sqrt(before) / jnp.sqrt(now), 0.0)
    move = jnp.where(
        live, jnp.sqrt(1.0 - before) - jnp.sqrt(before) * jnp.sqrt(1.0 - now) / jnp.sqrt(now), 0.0
    )
    tables = (frame_counts, along, keep, move)
    inner = (gaps - 1) * tokf
    out = denoise(
        0, gaps - 1, tables, gap_latent, lifted[:inner], lifted[tokf:], query_map, key_map
    )
    out = denoise(
        gaps - 1, 1, tables, gap_latent, lifted[inner:], following, query_map, key_map, into=out
    )
    return updated, out


def solution(mesh):
    fine = Mesh(mesh.devices.reshape(SIZES), AXES)
    mp = ("h", "c")
    placed = (
        P(FRAME, mp),
        P(None, FRAME, mp),
        P(None, FRAME, mp),
        P(FRAME, mp),
        P(mp, FRAME),
        P(FRAME, None, None, mp),
        P(mp, None, None),
        P(mp, None, None),
        P(FRAME),
        P(),
    )
    return jax.shard_map(
        on_device,
        mesh=fine,
        in_specs=placed,
        out_specs=(P(FRAME, mp), P(FRAME, None, None, mp)),
        check_vma=False,
    )
```

time: 678 us -> 173 us (0.26)
  the two profiles are of different devices: /device:TPU:2 before, /device:TPU:9 now
where the time goes in v1:
time: 173 us
  starting transfers between devices  56.7 us (33%)
  waiting for transfers between devices  56.2 us (32%)
  Pallas kernels  48 us (28%)
  local copies, waits for them, and re-layouts  6.72 us (4%)
  other arithmetic  3.28 us (2%)
  between operations  1.86 us (1%)
    pallas_call x2, Pallas kernels, denoise(): pl.pallas_call(functools.partial(gap_kernel, first, heads), grid_spec=plt...  33.6 us
    ppermute x3, waiting for transfers between devices, gather_weight(): lax.ppermute(weight, 'y', ring(4, d))  23.8 us
    ppermute x3, waiting for transfers between devices, on_device(): lax.ppermute(updated, 'z', ring(4, d))  12.3 us
    ppermute x1, starting transfers between devices, on_device(): following = lax.ppermute(initial, FRAME, down)  12 us
    all_to_all x1, waiting for transfers between devices, on_device(): parts = lax.all_to_all(parts, ('z', 'h'), 0, 0, tiled=False)  10.6 us
    ppermute x4, starting transfers between devices, gather_weight(): moved.append(lax.ppermute(table, ('x', 'c'), perm))  10.3 us
    ppermute x3, starting transfers between devices, on_device(): lax.ppermute(updated, 'z', ring(4, d))  9.83 us
    all_to_all x1, starting transfers between devices, on_device(): parts = lax.all_to_all(parts, ('z', 'h'), 0, 0, tiled=False)  8.1 us
  transfers between devices with their start and end apart: 18, of which 12 were waited for; matrix products, arithmetic and copies ran while one was open for 5% of the time, Pallas kernels for 17%

profile of v1, /device:TPU:9, one launch (start us, length us, event | category | flops | bytes accessed | tf_op | source)
XLA Modules:
  0.0 172.8 jit_solution(192704215815579627)
XLA Ops:
  0.6 3.5 %collective-permute-start = (bf16[2,256,1024]{2,1,0:T(8,128)(2,1)}, bf16[2,256,1024]{2,1,0:T(8,128)(2,1)}, u32[]{:S(2)}, u32[]{:S(2)}) collective-permute-start(bf16[2,256,1024]{2,1,0:T(8,128)(2,1)} %own.1), channel_id=1, source_target_pairs={{0,4},{4,8},{8,12},{12,16},{16,20},{20,24},{24,28},{28,32},{32,36}... | collective-permute-start | bytes 3145736 | tf_op jit(solution)/shard_map/ppermute | solution.py:264
  4.2 4.5 %collective-permute-start.1 = (bf16[2,256,1024]{2,1,0:T(8,128)(2,1)}, bf16[2,256,1024]{2,1,0:T(8,128)(2,1)}, u32[]{:S(2)}, u32[]{:S(2)}) collective-permute-start(bf16[2,256,1024]{2,1,0:T(8,128)(2,1)} %own.1), channel_id=1, source_target_pairs={{4,0},{8,4},{12,8},{16,12},{20,16},{24,20},{28,24},{32,28},{36,32}... | collective-permute-start | bytes 3145736 | tf_op jit(solution)/shard_map/ppermute | solution.py:265
  10.3 2.3 %collective-permute-start.10 = (bf16[1024,128]{1,0:T(8,128)(2,1)}, bf16[1024,128]{1,0:T(8,128)(2,1)S(1)}, u32[]{:S(2)}, u32[]{:S(2)}) collective-permute-start(bf16[1024,128]{1,0:T(8,128)(2,1)} %param.14), channel_id=1, source_target_pairs={{0,32},{16,48},{32,0},{48,16},{1,33},{17,49},{33,1},{49,17},{2,34}... | collective-permute-start | bytes 786440 | tf_op jit(solution)/shard_map/ppermute | solution.py:237
  12.6 23.8 %collective-permute-done.9 = bf16[1024,128]{1,0:T(8,128)(2,1)S(1)} collective-permute-done((bf16[1024,128]{1,0:T(8,128)(2,1)}, bf16[1024,128]{1,0:T(8,128)(2,1)S(1)}, u32[]{:S(2)}, u32[]{:S(2)}) %collective-permute-start.9) | collective-permute-done | bytes 262176 | tf_op jit(solution)/shard_map/ppermute | solution.py:237
  38.5 2.4 %collective-permute-start.15 = (bf16[4,1024,128]{2,1,0:T(8,128)(2,1)S(1)}, bf16[4,1024,128]{2,1,0:T(8,128)(2,1)S(1)}, u32[]{:S(2)}, u32[]{:S(2)}) collective-permute-start(bf16[4,1024,128]{2,1,0:T(8,128)(2,1)S(1)} %broadcast_select_fusion), channel_id=1, source_target_pairs={{0,192},{1,0},{64,1},{65,65},{128,64},{129,128},{192,129},{193,193... | collective-permute-start | bytes 3145736 | tf_op jit(solution)/shard_map/ppermute | solution.py:244
  40.9 2.9 %collective-permute-start.14 = (bf16[4,1024,128]{2,1,0:T(8,128)(2,1)S(1)}, bf16[4,1024,128]{2,1,0:T(8,128)(2,1)S(1)}, u32[]{:S(2)}, u32[]{:S(2)}) collective-permute-start(bf16[4,1024,128]{2,1,0:T(8,128)(2,1)S(1)} %broadcast_select_fusion), channel_id=1, source_target_pairs={{0,128},{1,192},{64,193},{65,1},{128,0},{129,64},{192,65},{193,129... | collective-permute-start | bytes 3145736 | tf_op jit(solution)/shard_map/ppermute | solution.py:244
  43.8 3.1 %collective-permute-start.13 = (bf16[4,1024,128]{2,1,0:T(8,128)(2,1)S(1)}, bf16[4,1024,128]{2,1,0:T(8,128)(2,1)}, u32[]{:S(2)}, u32[]{:S(2)}) collective-permute-start(bf16[4,1024,128]{2,1,0:T(8,128)(2,1)S(1)} %broadcast_select_fusion), channel_id=1, source_target_pairs={{0,64},{1,128},{64,129},{65,193},{128,192},{129,0},{192,1},{193,65... | collective-permute-start | bytes 3145736 | tf_op jit(solution)/shard_map/ppermute | solution.py:244
  46.9 1.9 %collective-permute-start.12 = (bf16[4,1024,128]{2,1,0:T(8,128)(2,1)S(1)}, bf16[4,1024,128]{2,1,0:T(8,128)(2,1)}, u32[]{:S(2)}, u32[]{:S(2)}) collective-permute-start(bf16[4,1024,128]{2,1,0:T(8,128)(2,1)S(1)} %broadcast_select_fusion), channel_id=1, source_target_pairs={{0,0},{1,64},{64,65},{65,129},{128,128},{129,192},{192,193},{193,1... | collective-permute-start | bytes 3145736 | tf_op jit(solution)/shard_map/ppermute | solution.py:244
  49.4 3.8 %collective-permute-done.1.nxt = bf16[2,256,1024]{2,1,0:T(8,128)(2,1)} collective-permute-done((bf16[2,256,1024]{2,1,0:T(8,128)(2,1)}, bf16[2,256,1024]{2,1,0:T(8,128)(2,1)}, u32[]{:S(2)}, u32[]{:S(2)}) %collective-permute-start.1) | collective-permute-done | bytes 1048608 | tf_op jit(solution)/shard_map/ppermute | solution.py:265
  53.3 6.1 %kf_attention.1.refs_0_ = bf16[64,1024]{1,0:T(8,128)(2,1)} custom-call(s32[2]{0:T(128)} %add_convert_fusion.edge, bf16[64,1024]{1,0:T(8,128)(2,1)} %q.1, bf16[2,64,1024]{2,1,0:T(8,128)(2,1)} %kv.1, bf16[2,256,1024]{2,1,0:T(8,128)(2,1)} %own.1, bf16[2,256,1024]{2,1,0:T(8,128)(2,1)} %collective-permute-done.prev, ...), custom_call_target="tpu_custom_call" | custom-call | flops 218103808 | bytes 3670016 | tf_op jit(solution)/shard_map/kf_attention/pallas_call | solution.py:60
  61.0 5.5 %collective-permute-start.4 = (bf16[64,1024]{1,0:T(8,128)(2,1)}, bf16[64,1024]{1,0:T(8,128)(2,1)S(1)}, u32[]{:S(2)}, u32[]{:S(2)}) collective-permute-start(bf16[64,1024]{1,0:T(8,128)(2,1)} %kf_attention.1.refs_0_), channel_id=1, source_target_pairs={{0,12},{4,0},{8,4},{12,8},{1,13},{5,1},{9,5},{13,9},{2,14},{6,2},{... | collective-permute-start | bytes 393224 | tf_op jit(solution)/shard_map/ppermute | solution.py:271
  66.5 3.1 %collective-permute-done.4.refs_3_ = bf16[64,1024]{1,0:T(8,128)(2,1)S(1)} collective-permute-done((bf16[64,1024]{1,0:T(8,128)(2,1)}, bf16[64,1024]{1,0:T(8,128)(2,1)S(1)}, u32[]{:S(2)}, u32[]{:S(2)}) %collective-permute-start.4) | collective-permute-done | bytes 131104 | tf_op jit(solution)/shard_map/ppermute | solution.py:271
  70.7 3.8 %collective-permute-done.3.refs_2_ = bf16[64,1024]{1,0:T(8,128)(2,1)S(1)} collective-permute-done((bf16[64,1024]{1,0:T(8,128)(2,1)}, bf16[64,1024]{1,0:T(8,128)(2,1)S(1)}, u32[]{:S(2)}, u32[]{:S(2)}) %collective-permute-start.3) | collective-permute-done | bytes 131104 | tf_op jit(solution)/shard_map/ppermute | solution.py:271
  74.5 3.2 %collective-permute-start.2 = (bf16[64,1024]{1,0:T(8,128)(2,1)}, bf16[64,1024]{1,0:T(8,128)(2,1)}, u32[]{:S(2)}, u32[]{:S(2)}) collective-permute-start(bf16[64,1024]{1,0:T(8,128)(2,1)} %kf_attention.1.refs_0_), channel_id=1, source_target_pairs={{0,4},{4,8},{8,12},{12,0},{1,5},{5,9},{9,13},{13,1},{2,6},{6,10},{... | collective-permute-start | bytes 393224 | tf_op jit(solution)/shard_map/ppermute | solution.py:271
  77.8 5.4 %collective-permute-done.2.refs_1_ = bf16[64,1024]{1,0:T(8,128)(2,1)} collective-permute-done((bf16[64,1024]{1,0:T(8,128)(2,1)}, bf16[64,1024]{1,0:T(8,128)(2,1)}, u32[]{:S(2)}, u32[]{:S(2)}) %collective-permute-start.2) | collective-permute-done | bytes 131104 | tf_op jit(solution)/shard_map/ppermute | solution.py:271
  83.1 3.4 %collective-permute-start.8 = (bf16[64,1024]{1,0:T(8,128)(2,1)S(1)}, bf16[64,1024]{1,0:T(8,128)(2,1)S(1)}, u32[]{:S(2)}, u32[]{:S(2)}) collective-permute-start(bf16[64,1024]{1,0:T(8,128)(2,1)S(1)} %collective-permute-done.4.refs_3_), channel_id=1, source_target_pairs={{0,1},{1,0},{2,3},{3,2},{4,5},{5,4},{6,7},{7,6},{8,9},{9,8},{10,11... | collective-permute-start | bytes 393224 | tf_op jit(solution)/shard_map/ppermute | solution.py:272
  93.1 6.5 %lift.1 = bf16[8,64,512]{2,1,0:T(8,128)(2,1)} custom-call(s32[9]{0:T(128)} %stack.82.info, bf16[64,1024]{1,0:T(8,128)(2,1)} %kf_attention.1.refs_0_, bf16[64,1024]{1,0:T(8,128)(2,1)} %collective-permute-done.2.refs_1_, bf16[64,1024]{1,0:T(8,128)(2,1)} %copy-done.5, bf16[64,1024]{1,0:T(8,128)(2,1)} %copy-done.4, bf16[64,1024]{1,0:T(8,128)(2,1)} %copy-done.3, ...), custom_call_target="tpu_custom_call" | custom-call | flops 1073741824 | bytes 5767168 | tf_op jit(solution)/shard_map/lift/pallas_call | solution.py:104
  99.6 8.1 %all-to-all-start = ((bf16[8,64,512]{2,1,0:T(8,128)(2,1)}), bf16[8,64,512]{2,1,0:T(8,128)(2,1)S(1)}, u32[]{:S(2)}, u32[]{:S(2)}) async-start(bf16[8,64,512]{2,1,0:T(8,128)(2,1)} %lift.1), calls=%async_computation | async-start | bytes 1048576 | tf_op jit(solution)/shard_map/all_to_all | solution.py:280
  110.1 10.6 %all-to-all-done.parts = bf16[8,64,512]{2,1,0:T(8,128)(2,1)S(1)} async-done(((bf16[8,64,512]{2,1,0:T(8,128)(2,1)}), bf16[8,64,512]{2,1,0:T(8,128)(2,1)S(1)}, u32[]{:S(2)}, u32[]{:S(2)}) %all-to-all-start) | async-done | bytes 524320 | tf_op jit(solution)/shard_map/all_to_all | solution.py:280
  121.5 1.9 %combine.1 = (bf16[64,2048]{1,0:T(8,128)(2,1)}, bf16[16,2048]{1,0:T(8,128)(2,1)}) custom-call(bf16[8,64,512]{2,1,0:T(8,128)(2,1)} %copy-done), custom_call_target="tpu_custom_call" | custom-call | flops 262144 | bytes 786432 | tf_op jit(solution)/shard_map/combine/pallas_call | solution.py:140
  123.3 12.0 %collective-permute-start.16 = (bf16[16,2048]{1,0:T(8,128)(2,1)}, bf16[16,2048]{1,0:T(8,128)(2,1)S(1)}, u32[]{:S(2)}, u32[]{:S(2)}) collective-permute-start(bf16[16,2048]{1,0:T(8,128)(2,1)} %get-tuple-element.5), channel_id=1, source_target_pairs={{4,0},{8,4},{12,8},{16,12},{20,16},{24,20},{28,24},{32,28},{36,32}... | collective-permute-start | bytes 196616 | tf_op jit(solution)/shard_map/ppermute | solution.py:284
  135.3 1.8 %fusion.5 = (bf16[48,2048]{1,0:T(8,128)(2,1)}, bf16[48,2048]{1,0:T(8,128)(2,1)}) fusion(bf16[64,2048]{1,0:T(8,128)(2,1)} %get-tuple-element.4), kind=kLoop, calls=%fused_computation.23 | loop fusion | bytes 786432 | tf_op jit(solution)/shard_map/slice | solution.py:300
  137.1 24.0 %denoise_0.1.rest_0_ = bf16[4,16,16,2048]{3,2,1,0:T(8,128)(2,1)} custom-call(s32[4]{0:T(128)} %count.3, f32[4,16]{1,0:T(4,128)} %broadcast_divide_fusion.along, f32[4,16]{1,0:T(4,128)} %get-tuple-element.9.keep, f32[4,16]{1,0:T(4,128)} %get-tuple-element.8.move, bf16[4,16,16,2048]{3,2,1,0:T(8,128)(2,1)} %latent.5, bf16[48,2048]{1,0:T(8,128)(2,1)} %get-tuple-element.7.left, ...), custom_call_target="tpu_custom_call" | custom-call | flops 2617245696 | bytes 6291456 | tf_op jit(solution)/shard_map/denoise_0/pallas_call | solution.py:209
  163.2 9.6 %denoise_3.1 = bf16[4,16,16,2048]{3,2,1,0:T(8,128)(2,1)} custom-call(s32[4]{0:T(128)} %count.3, f32[4,16]{1,0:T(4,128)} %broadcast_divide_fusion.along, f32[4,16]{1,0:T(4,128)} %get-tuple-element.9.keep, f32[4,16]{1,0:T(4,128)} %get-tuple-element.8.move, bf16[4,16,16,2048]{3,2,1,0:T(8,128)(2,1)} %latent.5, ...), custom_call_target="tpu_custom_call", output_to_operand_aliasing={{}: (9, {})} | custom-call | flops 872415232 | bytes 2097152 | tf_op jit(solution)/shard_map/denoise_3/pallas_call | solution.py:209
  (51 shorter events, 17.8 us)
Async XLA Ops:
  0.6 46.2 %collective-permute-start = (bf16[2,256,1024]{2,1,0:T(8,128)(2,1)}, bf16[2,256,1024]{2,1,0:T(8,128)(2,1)}, u32[]{:S(2)}, u32[]{:S(2)}) collective-permute-start(bf16[2,256,1024]{2,1,0:T(8,128)(2,1)} %own.1), channel_id=1, source_target_pairs={{0,4},{4,8},{8,12},{12,16},{16,20},{20,24},{24,28},{28,32},{32,36}... | collective-permute-start | bytes 3145736 | tf_op jit(solution)/shard_map/ppermute | solution.py:264
  4.2 49.1 %collective-permute-start.1 = (bf16[2,256,1024]{2,1,0:T(8,128)(2,1)}, bf16[2,256,1024]{2,1,0:T(8,128)(2,1)}, u32[]{:S(2)}, u32[]{:S(2)}) collective-permute-start(bf16[2,256,1024]{2,1,0:T(8,128)(2,1)} %own.1), channel_id=1, source_target_pairs={{4,0},{8,4},{12,8},{16,12},{20,16},{24,20},{28,24},{32,28},{36,32}... | collective-permute-start | bytes 3145736 | tf_op jit(solution)/shard_map/ppermute | solution.py:265
  8.7 27.8 %collective-permute-start.9 = (bf16[1024,128]{1,0:T(8,128)(2,1)}, bf16[1024,128]{1,0:T(8,128)(2,1)S(1)}, u32[]{:S(2)}, u32[]{:S(2)}) collective-permute-start(bf16[1024,128]{1,0:T(8,128)(2,1)} %param.14), channel_id=1, source_target_pairs={{0,16},{16,32},{32,48},{48,0},{1,17},{17,33},{33,49},{49,1},{2,18}... | collective-permute-start | bytes 786440 | tf_op jit(solution)/shard_map/ppermute | solution.py:237
  10.1 26.4 %collective-permute-start.11 = (bf16[1024,128]{1,0:T(8,128)(2,1)}, bf16[1024,128]{1,0:T(8,128)(2,1)S(1)}, u32[]{:S(2)}, u32[]{:S(2)}) collective-permute-start(bf16[1024,128]{1,0:T(8,128)(2,1)} %param.14), channel_id=1, source_target_pairs={{0,48},{16,0},{32,16},{48,32},{1,49},{17,1},{33,17},{49,33},{2,50}... | collective-permute-start | bytes 786440 | tf_op jit(solution)/shard_map/ppermute | solution.py:237
  10.3 26.2 %collective-permute-start.10 = (bf16[1024,128]{1,0:T(8,128)(2,1)}, bf16[1024,128]{1,0:T(8,128)(2,1)S(1)}, u32[]{:S(2)}, u32[]{:S(2)}) collective-permute-start(bf16[1024,128]{1,0:T(8,128)(2,1)} %param.14), channel_id=1, source_target_pairs={{0,32},{16,48},{32,0},{48,16},{1,33},{17,49},{33,1},{49,17},{2,34}... | collective-permute-start | bytes 786440 | tf_op jit(solution)/shard_map/ppermute | solution.py:237
  38.5 52.7 %collective-permute-start.15 = (bf16[4,1024,128]{2,1,0:T(8,128)(2,1)S(1)}, bf16[4,1024,128]{2,1,0:T(8,128)(2,1)S(1)}, u32[]{:S(2)}, u32[]{:S(2)}) collective-permute-start(bf16[4,1024,128]{2,1,0:T(8,128)(2,1)S(1)} %broadcast_select_fusion), channel_id=1, source_target_pairs={{0,192},{1,0},{64,1},{65,65},{128,64},{129,128},{192,129},{193,193... | collective-permute-start | bytes 3145736 | tf_op jit(solution)/shard_map/ppermute | solution.py:244
  40.9 50.3 %collective-permute-start.14 = (bf16[4,1024,128]{2,1,0:T(8,128)(2,1)S(1)}, bf16[4,1024,128]{2,1,0:T(8,128)(2,1)S(1)}, u32[]{:S(2)}, u32[]{:S(2)}) collective-permute-start(bf16[4,1024,128]{2,1,0:T(8,128)(2,1)S(1)} %broadcast_select_fusion), channel_id=1, source_target_pairs={{0,128},{1,192},{64,193},{65,1},{128,0},{129,64},{192,65},{193,129... | collective-permute-start | bytes 3145736 | tf_op jit(solution)/shard_map/ppermute | solution.py:244
  43.8 49.0 %collective-permute-start.13 = (bf16[4,1024,128]{2,1,0:T(8,128)(2,1)S(1)}, bf16[4,1024,128]{2,1,0:T(8,128)(2,1)}, u32[]{:S(2)}, u32[]{:S(2)}) collective-permute-start(bf16[4,1024,128]{2,1,0:T(8,128)(2,1)S(1)} %broadcast_select_fusion), channel_id=1, source_target_pairs={{0,64},{1,128},{64,129},{65,193},{128,192},{129,0},{192,1},{193,65... | collective-permute-start | bytes 3145736 | tf_op jit(solution)/shard_map/ppermute | solution.py:244
  46.9 46.2 %collective-permute-start.12 = (bf16[4,1024,128]{2,1,0:T(8,128)(2,1)S(1)}, bf16[4,1024,128]{2,1,0:T(8,128)(2,1)}, u32[]{:S(2)}, u32[]{:S(2)}) collective-permute-start(bf16[4,1024,128]{2,1,0:T(8,128)(2,1)S(1)} %broadcast_select_fusion), channel_id=1, source_target_pairs={{0,0},{1,64},{64,65},{65,129},{128,128},{129,192},{192,193},{193,1... | collective-permute-start | bytes 3145736 | tf_op jit(solution)/shard_map/ppermute | solution.py:244
  59.3 49.4 %copy-start.9 = (s32[4]{0:T(128)S(1)}, s32[4]{0:T(128)}, u32[]{:S(2)}) copy-start(s32[4]{0:T(128)} %count.3) | copy-start | bytes 52
  59.4 1.7 collective-permute-start.5
  61.0 32.0 %copy-start.3 = (bf16[64,1024]{1,0:T(8,128)(2,1)}, bf16[64,1024]{1,0:T(8,128)(2,1)S(1)}, u32[]{:S(2)}) copy-start(bf16[64,1024]{1,0:T(8,128)(2,1)S(1)} %collective-permute-done.5.refs_4_) | copy-start | bytes 393220
  61.0 8.5 %collective-permute-start.4 = (bf16[64,1024]{1,0:T(8,128)(2,1)}, bf16[64,1024]{1,0:T(8,128)(2,1)S(1)}, u32[]{:S(2)}, u32[]{:S(2)}) collective-permute-start(bf16[64,1024]{1,0:T(8,128)(2,1)} %kf_attention.1.refs_0_), channel_id=1, source_target_pairs={{0,12},{4,0},{8,4},{12,8},{1,13},{5,1},{9,5},{13,9},{2,14},{6,2},{... | collective-permute-start | bytes 393224 | tf_op jit(solution)/shard_map/ppermute | solution.py:271
  69.6 23.5 %copy-start.4 = (bf16[64,1024]{1,0:T(8,128)(2,1)}, bf16[64,1024]{1,0:T(8,128)(2,1)S(1)}, u32[]{:S(2)}) copy-start(bf16[64,1024]{1,0:T(8,128)(2,1)S(1)} %collective-permute-done.4.refs_3_) | copy-start | bytes 393220
  69.6 4.9 %collective-permute-start.3 = (bf16[64,1024]{1,0:T(8,128)(2,1)}, bf16[64,1024]{1,0:T(8,128)(2,1)S(1)}, u32[]{:S(2)}, u32[]{:S(2)}) collective-permute-start(bf16[64,1024]{1,0:T(8,128)(2,1)} %kf_attention.1.refs_0_), channel_id=1, source_target_pairs={{0,8},{4,12},{8,0},{12,4},{1,9},{5,13},{9,1},{13,5},{2,10},{6,14},... | collective-permute-start | bytes 393224 | tf_op jit(solution)/shard_map/ppermute | solution.py:271
  74.5 18.5 %copy-start.5 = (bf16[64,1024]{1,0:T(8,128)(2,1)}, bf16[64,1024]{1,0:T(8,128)(2,1)S(1)}, u32[]{:S(2)}) copy-start(bf16[64,1024]{1,0:T(8,128)(2,1)S(1)} %collective-permute-done.3.refs_2_) | copy-start | bytes 393220
  74.5 8.6 %collective-permute-start.2 = (bf16[64,1024]{1,0:T(8,128)(2,1)}, bf16[64,1024]{1,0:T(8,128)(2,1)}, u32[]{:S(2)}, u32[]{:S(2)}) collective-permute-start(bf16[64,1024]{1,0:T(8,128)(2,1)} %kf_attention.1.refs_0_), channel_id=1, source_target_pairs={{0,4},{4,8},{8,12},{12,0},{1,5},{5,9},{9,13},{13,1},{2,6},{6,10},{... | collective-permute-start | bytes 393224 | tf_op jit(solution)/shard_map/ppermute | solution.py:271
  83.1 4.4 %collective-permute-start.8 = (bf16[64,1024]{1,0:T(8,128)(2,1)S(1)}, bf16[64,1024]{1,0:T(8,128)(2,1)S(1)}, u32[]{:S(2)}, u32[]{:S(2)}) collective-permute-start(bf16[64,1024]{1,0:T(8,128)(2,1)S(1)} %collective-permute-done.4.refs_3_), channel_id=1, source_target_pairs={{0,1},{1,0},{2,3},{3,2},{4,5},{5,4},{6,7},{7,6},{8,9},{9,8},{10,11... | collective-permute-start | bytes 393224 | tf_op jit(solution)/shard_map/ppermute | solution.py:272
  87.5 1.3 collective-permute-start.7
  89.5 1.7 collective-permute-start.6
  91.2 1.8 %copy-start.1 = (bf16[4,1024,128]{2,1,0:T(8,128)(2,1)}, bf16[4,1024,128]{2,1,0:T(8,128)(2,1)S(1)}, u32[]{:S(2)}) copy-start(bf16[4,1024,128]{2,1,0:T(8,128)(2,1)S(1)} %collective-permute-done.15.refs_11_) | copy-start | bytes 3145732
  91.2 1.9 %copy-start.2 = (bf16[4,1024,128]{2,1,0:T(8,128)(2,1)}, bf16[4,1024,128]{2,1,0:T(8,128)(2,1)S(1)}, u32[]{:S(2)}) copy-start(bf16[4,1024,128]{2,1,0:T(8,128)(2,1)S(1)} %collective-permute-done.14.refs_10_) | copy-start | bytes 3145732
  99.6 21.1 %all-to-all-start = ((bf16[8,64,512]{2,1,0:T(8,128)(2,1)}), bf16[8,64,512]{2,1,0:T(8,128)(2,1)S(1)}, u32[]{:S(2)}, u32[]{:S(2)}) async-start(bf16[8,64,512]{2,1,0:T(8,128)(2,1)} %lift.1), calls=%async_computation | async-start | bytes 1048576 | tf_op jit(solution)/shard_map/all_to_all | solution.py:280
  123.3 39.2 %collective-permute-start.16 = (bf16[16,2048]{1,0:T(8,128)(2,1)}, bf16[16,2048]{1,0:T(8,128)(2,1)S(1)}, u32[]{:S(2)}, u32[]{:S(2)}) collective-permute-start(bf16[16,2048]{1,0:T(8,128)(2,1)} %get-tuple-element.5), channel_id=1, source_target_pairs={{4,0},{8,4},{12,8},{16,12},{20,16},{24,20},{28,24},{32,28},{36,32}... | collective-permute-start | bytes 196616 | tf_op jit(solution)/shard_map/ppermute | solution.py:284
  (4 other events, 3.4 us)

commit v2 on v1

v2 whole, which is shorter than its diff:
```python
import functools
import math

import jax
import jax.numpy as jnp
from jax import lax
from jax.experimental import pallas as pl
from jax.experimental.pallas import tpu as pltpu
from jax.sharding import Mesh
from jax.sharding import PartitionSpec as P

HD = 128
STRIDE = 200
NEG = -1e30
BF = jnp.bfloat16
F32 = jnp.float32
SCALE = HD ** (-0.5)
SIZES = (4, 4, 4, 2, 2)
AXES = ("x", "y", "z", "h", "c")
FRAME = ("x", "y", "z")
N_FRAME = 64


def nt(a, b):
    return lax.dot_general(a, b, (((1,), (1,)), ((), ())), preferred_element_type=F32)


def tn(a, b):
    return lax.dot_general(a, b, (((0,), (0,)), ((), ())), preferred_element_type=F32)


def nn(a, b):
    return jnp.dot(a, b, preferred_element_type=F32)


def part_of(query, pairs, cols):
    scores = [nt(query, kv[0, :, cols]) for kv in pairs]
    top = functools.reduce(jnp.maximum, [jnp.max(s, axis=1, keepdims=True) for s in scores])
    probs = [jnp.exp((s - top) * SCALE) for s in scores]
    total = sum(jnp.sum(p, axis=1, keepdims=True) for p in probs)
    mixed = sum(nn(p.astype(BF), kv[1, :, cols]) for p, kv in zip(probs, pairs))
    return mixed * (1.0 / total), top * SCALE + jnp.log(total)


def own_kernel(q, kv, own, latent, out, logs, kept):
    step = pl.program_id(0)
    lane = lax.broadcasted_iota(jnp.int32, logs.shape, 1)

    @pl.when(step == 0)
    def _():
        logs[...] = jnp.zeros(logs.shape, F32)

    count = q.shape[1] // HD
    for h in range(count):
        cols = slice(h * HD, (h + 1) * HD)
        mixed, log = part_of(q[:, cols], (own, kv), cols)
        out[:, cols] = mixed
        logs[...] = jnp.where(lane == step * count + h, log, logs[...])
    kept[...] = latent[...]


def own_part(q, kv, own, latent):
    rows, width = q.shape
    ctx = own.shape[1]
    keys = kv.shape[1] + ctx
    step = 2 * HD
    flat = pl.BlockSpec((rows, step), lambda i: (0, i))
    return pl.pallas_call(
        own_kernel,
        grid=(width // step,),
        in_specs=[
            flat,
            pl.BlockSpec((2, rows, step), lambda i: (0, 0, i)),
            pl.BlockSpec((2, ctx, step), lambda i: (0, 0, i)),
            flat,
        ],
        out_specs=(flat, pl.BlockSpec((rows, HD), lambda i: (0, 0)), flat),
        out_shape=(
            jax.ShapeDtypeStruct((rows, width), F32),
            jax.ShapeDtypeStruct((rows, HD), F32),
            jax.ShapeDtypeStruct((rows, width), BF),
        ),
        cost_estimate=pl.CostEstimate(
            flops=4 * rows * width * keys,
            bytes_accessed=4 * keys * width + 6 * rows * width,
            transcendentals=rows * (width // HD) * keys,
        ),
        compiler_params=pltpu.CompilerParams(vmem_limit_bytes=56 << 20),
        name="own_part",
    )(q, kv, own, latent)


def far_kernel(q_a, q_b, own, out_a, out_b):
    rows, width = q_a.shape
    heads = width // HD
    lane = lax.broadcasted_iota(jnp.int32, (2 * rows, HD), 1)
    logs = jnp.zeros((2 * rows, HD), F32)
    for h in range(heads):
        cols = slice(h * HD, (h + 1) * HD)
        query = jnp.concatenate([q_a[:, cols], q_b[:, cols]], axis=0)
        mixed, log = part_of(query, (own,), cols)
        out_a[:, cols] = mixed[:rows].astype(BF)
        out_b[:, cols] = mixed[rows:].astype(BF)
        for k in range(3):
            piece = log.astype(BF).astype(F32)
            logs = jnp.where(lane == k * heads + h, piece, logs)
            log = log - piece
    out_a[:, width:] = logs[:rows].astype(BF)
    out_b[:, width:] = logs[rows:].astype(BF)


def far_parts(q_a, q_b, own):
    rows, width = q_a.shape
    keys = own.shape[1]
    shape = jax.ShapeDtypeStruct((rows, width + HD), BF)
    return pl.pallas_call(
        far_kernel,
        out_shape=(shape, shape),
        cost_estimate=pl.CostEstimate(
            flops=8 * rows * width * keys,
            bytes_accessed=4 * keys * width + 8 * rows * width,
            transcendentals=2 * rows * (width // HD) * keys,
        ),
        compiler_params=pltpu.CompilerParams(vmem_limit_bytes=16 << 20),
        name="far_parts",
    )(q_a, q_b, own)


def join_kernel(edge, latent, own, stat, before, after, out, moving):
    rows, width = latent.shape
    heads = width // HD

    def log_of(part, there):
        logs = part[:, width:].astype(F32)
        logs = logs + pltpu.roll(logs, HD - heads, 1) + pltpu.roll(logs, HD - 2 * heads, 1)
        return jnp.where(there, logs, NEG)

    logs = (stat[...], log_of(before, edge[0] > 0), log_of(after, edge[1] > 0))
    top = functools.reduce(jnp.maximum, logs)
    share = [jnp.exp(v - top) for v in logs]
    inverse = 1.0 / (share[0] + share[1] + share[2])
    share = [v * inverse for v in share]
    for h in range(heads):
        cols = slice(h * HD, (h + 1) * HD)
        one = slice(h, h + 1)
        attn = (
            own[:, cols] * share[0][:, one]
            + before[:, cols].astype(F32) * share[1][:, one]
            + after[:, cols].astype(F32) * share[2][:, one]
        )
        total = (latent[:, cols].astype(F32) + attn).astype(BF)
        out[:, cols] = total
        moving[:, cols] = total


def join(edge, latent, own, stat, before, after):
    rows, width = latent.shape
    vmem = pl.BlockSpec(memory_space=pltpu.VMEM)
    return pl.pallas_call(
        join_kernel,
        in_specs=[pl.BlockSpec(memory_space=pltpu.SMEM)] + [vmem] * 5,
        out_shape=(jax.ShapeDtypeStruct((rows, width), BF),) * 2,
        cost_estimate=pl.CostEstimate(
            flops=8 * rows * width, bytes_accessed=12 * rows * width, transcendentals=4 * rows * HD
        ),
        compiler_params=pltpu.CompilerParams(vmem_limit_bytes=56 << 20),
        name="join",
    )(edge, latent, own, stat, before, after)


def lift_kernel(info, *refs):
    acts, pieces = refs[0:4], refs[4:8]
    keep, send, rows = refs[8:]
    x, y, z, c = info[0], info[1], info[2], info[3]
    frame_rows = acts[0].shape[0]
    for d in range(4):
        rows[d * frame_rows : (d + 1) * frame_rows, :] = acts[d][...]
    for e in range(4):
        for pair in range(2):
            total = nn(
                rows[...],
                jnp.concatenate([pieces[e][2 * pair], pieces[e][2 * pair + 1]], axis=1),
            )
            for k in range(2):
                d = 2 * pair + k
                head_x = lax.rem(x + 4 - jnp.where(c == 0, e, d), 4)
                head_y = lax.rem(y + 4 - jnp.where(c == 0, d, e), 4)
                mine = lax.rem(head_x, 2) == c
                cols = pl.ds(pl.multiple_of(head_y * HD, HD), HD)

                def put(out, cast):
                    for f in range(4):
                        to = lax.rem(z + 4 - f, 4) * 2 + head_x // 2
                        part = total[f * frame_rows : (f + 1) * frame_rows]
                        out[to, :, cols] = cast(part[:, k * HD : (k + 1) * HD])

                @pl.when(mine)
                def _():
                    put(keep, lambda v: v)

                @pl.when(jnp.logical_not(mine))
                def _():
                    put(send, lambda v: v.astype(BF))


def lift(info, acts, pieces):
    rows, width = acts[0].shape
    vmem = pl.BlockSpec(memory_space=pltpu.VMEM)
    return pl.pallas_call(
        lift_kernel,
        in_specs=[pl.BlockSpec(memory_space=pltpu.SMEM)] + [vmem] * 8,
        out_shape=(
            jax.ShapeDtypeStruct((8, rows, 4 * HD), F32),
            jax.ShapeDtypeStruct((8, rows, 4 * HD), BF),
        ),
        scratch_shapes=[pltpu.VMEM((4 * rows, width), BF)],
        compiler_params=pltpu.CompilerParams(vmem_limit_bytes=24 << 20),
        cost_estimate=pl.CostEstimate(
            flops=2 * 4 * rows * width * 16 * HD,
            bytes_accessed=2 * (16 * width * HD + 4 * rows * width + 48 * rows * HD),
            transcendentals=0,
        ),
        name="lift",
    )(info, *acts, *pieces)


def combine_kernel(parts, out, first):
    for y in range(4):
        cols = slice(y * HD, (y + 1) * HD)
        for z in range(4):
            place = slice((y * 4 + z) * HD, (y * 4 + z + 1) * HD)
            total = parts[2 * z, :, cols].astype(F32) + parts[2 * z + 1, :, cols].astype(F32)
            total = total.astype(BF)
            out[:, place] = total
            first[:, place] = total[: first.shape[0]]


def combine(parts, tokf):
    rows = parts.shape[1]
    width = 4 * parts.shape[2]
    return pl.pallas_call(
        combine_kernel,
        out_shape=(
            jax.ShapeDtypeStruct((rows, width), BF),
            jax.ShapeDtypeStruct((tokf, width), BF),
        ),
        cost_estimate=pl.CostEstimate(
            flops=2 * rows * width, bytes_accessed=6 * rows * width, transcendentals=0
        ),
        compiler_params=pltpu.CompilerParams(vmem_limit_bytes=16 << 20),
        name="combine",
    )(parts)


def gap_kernel(first, count, along, keep, move, latent, left, right, qmap, kmap, *rest):
    out = rest[-1]
    gap = first + pl.program_id(0)
    heads = qmap.shape[0]
    frames, tokf = latent.shape[1], latent.shape[2]
    toks = frames * tokf
    live = count[gap] * tokf
    bias = jnp.where(lax.broadcasted_iota(jnp.int32, (toks, 1), 0) < live, 0.0, NEG).astype(F32)

    def map_rows(h):
        cols = slice(h * HD, (h + 1) * HD)
        lo, hi = left[:, cols], right[:, cols]
        lo32, hi32 = lo.astype(F32), hi.astype(F32)
        tokens = [
            (
                latent[0, j, :, cols].astype(F32)
                + (1.0 - along[gap, j]) * lo32
                + along[gap, j] * hi32
            ).astype(BF)
            for j in range(frames)
        ]
        values = jnp.concatenate(tokens + [lo, hi], axis=0)
        mapped = nn(values, jnp.concatenate([qmap[h], kmap[h]], axis=1)).astype(BF)
        return values, mapped[:toks, :HD], mapped[:, HD:]

    def score(values, query, key):
        scores = nt(key, query)
        return values, jnp.concatenate([scores[:toks] + bias, scores[toks:]], axis=0)

    def finish(h, values, scores):
        cols = slice(h * HD, (h + 1) * HD)
        top = jnp.max(scores, axis=0, keepdims=True)
        probs = jnp.exp2((scores - top) * (SCALE * math.log2(math.e)))
        total = jnp.sum(probs, axis=0, keepdims=True)
        mixed = tn(values, probs.astype(BF))
        guess = jnp.transpose(mixed * (1.0 / total))
        for j in range(frames):
            rows = slice(j * tokf, (j + 1) * tokf)
            out[0, j, :, cols] = (
                latent[0, j, :, cols].astype(F32) * keep[gap, j] + guess[rows] * move[gap, j]
            ).astype(BF)

    mapped, scored = {}, {}
    for t in range(heads + 2):
        if t < heads:
            mapped[t] = map_rows(t)
        if 0 <= t - 1 < heads:
            scored[t - 1] = score(*mapped.pop(t - 1))
        if 0 <= t - 2 < heads:
            finish(t - 2, *scored.pop(t - 2))


def denoise(first, gaps, tables, latent, left, right, right_at, qmap, kmap, into=None):
    _, frames, tokf, width = latent.shape
    heads = width // HD
    spot = pl.BlockSpec((1, frames, tokf, width), lambda g, *s: (first + g, 0, 0, 0))
    before = pl.BlockSpec((tokf, width), lambda g, *s: (first + g, 0))
    after = pl.BlockSpec((tokf, width), lambda g, *s: (right_at + g, 0))
    maps = pl.BlockSpec((heads, HD, HD), lambda g, *s: (0, 0, 0))
    extra = [] if into is None else [into]
    specs = [spot, before, after, maps, maps] + [pl.BlockSpec(memory_space=pl.ANY)] * len(extra)
    toks = frames * tokf
    return pl.pallas_call(
        functools.partial(gap_kernel, first),
        grid_spec=pltpu.PrefetchScalarGridSpec(
            num_scalar_prefetch=4, grid=(gaps,), in_specs=specs, out_specs=spot
        ),
        out_shape=jax.ShapeDtypeStruct(latent.shape, BF),
        input_output_aliases={9: 0} if extra else {},
        compiler_params=pltpu.CompilerParams(vmem_limit_bytes=52 << 20),
        cost_estimate=pl.CostEstimate(
            flops=gaps * 2 * toks * width * (2 * HD + 2 * (toks + 2 * tokf)),
            bytes_accessed=4 * gaps * toks * width,
            transcendentals=gaps * heads * toks * (toks + 2 * tokf),
        ),
        name=f"denoise_{first}",
    )(*tables, latent, left, right, qmap, kmap, *extra)


def signal_level(step):
    return jnp.cos((step / 1000.0 + 0.008) / 1.008 * (math.pi / 2)) ** 2


def ring(size, by):
    return [(i, (i + by) % size) for i in range(size)]


def crossed(value, by, swap):
    perm = []
    for a in range(4):
        for b in range(4):
            for core in range(2):
                if (core == 0) != swap:
                    to = (a, (b + by) % 4)
                else:
                    to = ((a + by) % 4, b)
                perm.append(((a * 4 + b) * 2 + core, (to[0] * 4 + to[1]) * 2 + core))
    return lax.ppermute(value, ("x", "y", "c"), perm)


def on_device(
    kf_query,
    kf_kv,
    cache_kv,
    kf_latent,
    lift_weight,
    gap_latent,
    query_map,
    key_map,
    frame_counts,
    noise_step,
):
    x, y, z, h, c = (lax.axis_index(a) for a in AXES)
    frame = (x * 4 + y) * 4 + z
    up = [(i, i + 1) for i in range(N_FRAME - 1)]
    down = [(j, i) for i, j in up]
    q_prev = lax.ppermute(kf_query, FRAME, up)
    q_next = lax.ppermute(kf_query, FRAME, down)
    line = jnp.stack([lift_weight] + [crossed(lift_weight, d, False) for d in (1, 2, 3)])

    edge = jnp.stack([frame > 0, frame < N_FRAME - 1]).astype(jnp.int32)
    own, stat, latent = own_part(kf_query, kf_kv, cache_kv, kf_latent)
    q_prev, q_next, line, _ = lax.optimization_barrier((q_prev, q_next, line, own))
    to_prev, to_next = far_parts(q_prev, q_next, cache_kv)
    after = lax.ppermute(to_prev, FRAME, down)
    before = lax.ppermute(to_next, FRAME, up)
    pieces = [line] + [crossed(line, e, True) for e in (1, 2, 3)]
    updated, moving = join(edge, latent, own, stat, before, after)

    acts = [moving] + [lax.ppermute(moving, "z", ring(4, d)) for d in (1, 2, 3)]
    info = jnp.stack([x, y, z, c]).astype(jnp.int32)
    keep, send = lift(info, acts, pieces)
    parts = (keep + lax.ppermute(send, "c", ring(2, 1)).astype(F32)).astype(BF)
    parts = lax.all_to_all(parts, ("z", "h"), 0, 0, tiled=False)

    gaps, frames, tokf, width = gap_latent.shape
    lifted, initial = combine(parts, tokf)
    following = lax.ppermute(initial, FRAME, down)

    step = noise_step[0].astype(F32)
    now = signal_level(step)
    then = signal_level(step - STRIDE)
    slots = jnp.arange(frames, dtype=jnp.int32)[None]
    counts = frame_counts[:, None]
    along = (slots + 1).astype(F32) / (counts + 1).astype(F32)
    live = slots < counts
    keep = jnp.where(live, jnp.sqrt(then) / jnp.sqrt(now), 0.0)
    move = jnp.where(
        live, jnp.sqrt(1.0 - then) - jnp.sqrt(then) * jnp.sqrt(1.0 - now) / jnp.sqrt(now), 0.0
    )
    tables = (frame_counts, along, keep, move)
    last = gaps - 1
    out = denoise(0, last, tables, gap_latent, lifted, lifted, 1, query_map, key_map)
    out = denoise(
        last, 1, tables, gap_latent, lifted, following, 0, query_map, key_map, into=out
    )
    return updated, out


def solution(mesh):
    fine = Mesh(mesh.devices.reshape(SIZES), AXES)
    mp = ("h", "c")
    placed = (
        P(FRAME, mp),
        P(None, FRAME, mp),
        P(None, FRAME, mp),
        P(FRAME, mp),
        P(mp, FRAME),
        P(FRAME, None, None, mp),
        P(mp, None, None),
        P(mp, None, None),
        P(FRAME),
        P(),
    )
    return jax.shard_map(
        on_device,
        mesh=fine,
        in_specs=placed,
        out_specs=(P(FRAME, mp), P(FRAME, None, None, mp)),
        check_vma=False,
    )
```

time: 173 us -> 120 us (0.69)
  the two profiles are of different devices: /device:TPU:9 before, /device:TPU:2 now
where the time goes in v2:
time: 120 us
  starting transfers between devices  43.5 us (36%)
  waiting for transfers between devices  36.1 us (30%)
  Pallas kernels  33.7 us (28%)
  other arithmetic  2.95 us (2%)
  between operations  1.88 us (2%)
  local copies, waits for them, and re-layouts  1.62 us (1%)
    pallas_call x2, Pallas kernels, denoise(): pl.pallas_call(functools.partial(gap_kernel, first), grid_spec=pltpu.Pref...  20.4 us
    ppermute x3, waiting for transfers between devices, on_device(): acts = [moving] + [lax.ppermute(moving, 'z', ring(4, d)) for d in (1, 2, 3)]  14.2 us
    all_to_all x1, waiting for transfers between devices, on_device(): parts = lax.all_to_all(parts, ('z', 'h'), 0, 0, tiled=False)  12.9 us
    ppermute x6, starting transfers between devices, crossed(): return lax.ppermute(value, ('x', 'y', 'c'), perm)  9.41 us
    ppermute x1, starting transfers between devices, on_device(): after = lax.ppermute(to_prev, FRAME, down)  8.73 us
    ppermute x1, starting transfers between devices, on_device(): following = lax.ppermute(initial, FRAME, down)  8.25 us
    ppermute x1, starting transfers between devices, on_device(): q_next = lax.ppermute(kf_query, FRAME, down)  6.98 us
    all_to_all x1, starting transfers between devices, on_device(): parts = lax.all_to_all(parts, ('z', 'h'), 0, 0, tiled=False)  5.77 us
  transfers between devices with their start and end apart: 16, of which 7 were waited for; matrix products, arithmetic and copies ran while one was open for 2% of the time, Pallas kernels for 18%

profile of v2, /device:TPU:2, one launch (start us, length us, event | category | flops | bytes accessed | tf_op | source)
XLA Modules:
  0.0 119.8 jit_solution(15011322019240780962)
XLA Ops:
  0.6 1.7 %collective-permute-start.2 = (bf16[1024,128]{1,0:T(8,128)(2,1)}, bf16[1024,128]{1,0:T(8,128)(2,1)S(1)}, u32[]{:S(2)}, u32[]{:S(2)}) collective-permute-start(bf16[1024,128]{1,0:T(8,128)(2,1)} %param.14), channel_id=1, source_target_pairs={{0,16},{1,65},{16,32},{17,81},{32,48},{33,97},{48,0},{49,113},{64,... | collective-permute-start | bytes 786440 | tf_op jit(solution)/shard_map/ppermute | solution.py:352
  2.3 1.7 %collective-permute-start.4 = (bf16[1024,128]{1,0:T(8,128)(2,1)}, bf16[1024,128]{1,0:T(8,128)(2,1)S(1)}, u32[]{:S(2)}, u32[]{:S(2)}) collective-permute-start(bf16[1024,128]{1,0:T(8,128)(2,1)} %param.14), channel_id=1, source_target_pairs={{0,48},{1,193},{16,0},{17,209},{32,16},{33,225},{48,32},{49,241},{... | collective-permute-start | bytes 786440 | tf_op jit(solution)/shard_map/ppermute | solution.py:352
  4.0 2.0 %collective-permute-start.3 = (bf16[1024,128]{1,0:T(8,128)(2,1)}, bf16[1024,128]{1,0:T(8,128)(2,1)S(1)}, u32[]{:S(2)}, u32[]{:S(2)}) collective-permute-start(bf16[1024,128]{1,0:T(8,128)(2,1)} %param.14), channel_id=1, source_target_pairs={{0,32},{1,129},{16,48},{17,145},{32,0},{33,161},{48,16},{49,177},{... | collective-permute-start | bytes 786440 | tf_op jit(solution)/shard_map/ppermute | solution.py:352
  5.9 7.0 %collective-permute-start.1 = (bf16[64,1024]{1,0:T(8,128)(2,1)}, bf16[64,1024]{1,0:T(8,128)(2,1)S(1)}, u32[]{:S(2)}, u32[]{:S(2)}) collective-permute-start(bf16[64,1024]{1,0:T(8,128)(2,1)} %q.1), channel_id=1, source_target_pairs={{4,0},{8,4},{12,8},{16,12},{20,16},{24,20},{28,24},{32,28},{36,32}... | collective-permute-start | bytes 393224 | tf_op jit(solution)/shard_map/ppermute | solution.py:372
  12.9 1.9 %collective-permute-start = (bf16[64,1024]{1,0:T(8,128)(2,1)}, bf16[64,1024]{1,0:T(8,128)(2,1)S(1)}, u32[]{:S(2)}, u32[]{:S(2)}) collective-permute-start(bf16[64,1024]{1,0:T(8,128)(2,1)} %q.1), channel_id=1, source_target_pairs={{0,4},{4,8},{8,12},{12,16},{16,20},{20,24},{24,28},{28,32},{32,36}... | collective-permute-start | bytes 393224 | tf_op jit(solution)/shard_map/ppermute | solution.py:371
  14.9 4.7 %own_part.1 = (f32[64,1024]{1,0:T(8,128)}, f32[64,128]{1,0:T(8,128)}, bf16[64,1024]{1,0:T(8,128)(2,1)}) custom-call(bf16[64,1024]{1,0:T(8,128)(2,1)} %q.1, bf16[2,64,1024]{2,1,0:T(8,128)(2,1)} %kv.1, bf16[2,256,1024]{2,1,0:T(8,128)(2,1)} %own.3, bf16[64,1024]{1,0:T(8,128)(2,1)} %latent.3), custom_call_target="tpu_custom_call" | custom-call | flops 83886080 | bytes 1703936 | tf_op jit(solution)/shard_map/own_part/pallas_call | solution.py:68
  19.6 1.1 pad_maximum_fusion.refs_4_
  20.7 5.1 %collective-permute-done.q_a = bf16[64,1024]{1,0:T(8,128)(2,1)S(1)} collective-permute-done((bf16[64,1024]{1,0:T(8,128)(2,1)}, bf16[64,1024]{1,0:T(8,128)(2,1)S(1)}, u32[]{:S(2)}, u32[]{:S(2)}) %collective-permute-start) | collective-permute-done | bytes 131104 | tf_op jit(solution)/shard_map/ppermute | solution.py:371
  25.7 2.1 %collective-permute-start.11 = (bf16[4,1024,128]{2,1,0:T(8,128)(2,1)S(1)}, bf16[4,1024,128]{2,1,0:T(8,128)(2,1)}, u32[]{:S(2)}, u32[]{:S(2)}) collective-permute-start(bf16[4,1024,128]{2,1,0:T(8,128)(2,1)S(1)} %pad_maximum_fusion.refs_4_), channel_id=1, source_target_pairs={{0,128},{1,33},{16,144},{17,49},{32,160},{33,1},{48,176},{49,17},{... | collective-permute-start | bytes 3145736 | tf_op jit(solution)/shard_map/ppermute | solution.py:352
  27.8 2.1 %collective-permute-start.10 = (bf16[4,1024,128]{2,1,0:T(8,128)(2,1)S(1)}, bf16[4,1024,128]{2,1,0:T(8,128)(2,1)}, u32[]{:S(2)}, u32[]{:S(2)}) collective-permute-start(bf16[4,1024,128]{2,1,0:T(8,128)(2,1)S(1)} %pad_maximum_fusion.refs_4_), channel_id=1, source_target_pairs={{0,64},{1,17},{16,80},{17,33},{32,96},{33,49},{48,112},{49,1},{64,... | collective-permute-start | bytes 3145736 | tf_op jit(solution)/shard_map/ppermute | solution.py:352
  30.9 1.9 %collective-permute-start.5 = (bf16[64,1152]{1,0:T(8,128)(2,1)S(1)}, bf16[64,1152]{1,0:T(8,128)(2,1)S(1)}, u32[]{:S(2)}, u32[]{:S(2)}) collective-permute-start(bf16[64,1152]{1,0:T(8,128)(2,1)S(1)} %get-tuple-element.21), channel_id=1, source_target_pairs={{0,4},{4,8},{8,12},{12,16},{16,20},{20,24},{24,28},{28,32},{32,36}... | collective-permute-start | bytes 442376 | tf_op jit(solution)/shard_map/ppermute | solution.py:380
  32.8 8.7 %collective-permute-start.6 = (bf16[64,1152]{1,0:T(8,128)(2,1)S(1)}, bf16[64,1152]{1,0:T(8,128)(2,1)S(1)}, u32[]{:S(2)}, u32[]{:S(2)}) collective-permute-start(bf16[64,1152]{1,0:T(8,128)(2,1)S(1)} %get-tuple-element.22), channel_id=1, source_target_pairs={{4,0},{8,4},{12,8},{16,12},{20,16},{24,20},{28,24},{32,28},{36,32}... | collective-permute-start | bytes 442376 | tf_op jit(solution)/shard_map/ppermute | solution.py:379
  42.2 2.0 %collective-permute-done.5.before = bf16[64,1152]{1,0:T(8,128)(2,1)S(1)} collective-permute-done((bf16[64,1152]{1,0:T(8,128)(2,1)S(1)}, bf16[64,1152]{1,0:T(8,128)(2,1)S(1)}, u32[]{:S(2)}, u32[]{:S(2)}) %collective-permute-start.5) | collective-permute-done | bytes 147488 | tf_op jit(solution)/shard_map/ppermute | solution.py:380
  45.0 2.3 %join.1 = (bf16[64,1024]{1,0:T(8,128)(2,1)}, bf16[64,1024]{1,0:T(8,128)(2,1)}) custom-call(s32[2]{0:T(128)} %add_convert_fusion.1.edge, bf16[64,1024]{1,0:T(8,128)(2,1)} %get-tuple-element.16.latent, f32[64,1024]{1,0:T(8,128)} %get-tuple-element.17.own, f32[64,128]{1,0:T(8,128)} %get-tuple-element.18.stat, bf16[64,1152]{1,0:T(8,128)(2,1)} %copy-done.5, ...), custom_call_target="tpu_custom_call" | custom-call | flops 524288 | bytes 786432 | tf_op jit(solution)/shard_map/join/pallas_call | solution.py:159
  47.7 7.3 %collective-permute-done.9.refs_3_ = bf16[64,1024]{1,0:T(8,128)(2,1)S(1)} collective-permute-done((bf16[64,1024]{1,0:T(8,128)(2,1)}, bf16[64,1024]{1,0:T(8,128)(2,1)S(1)}, u32[]{:S(2)}, u32[]{:S(2)}) %collective-permute-start.9) | collective-permute-done | bytes 131104 | tf_op jit(solution)/shard_map/ppermute | solution.py:384
  55.1 1.5 %collective-permute-done.8.refs_2_ = bf16[64,1024]{1,0:T(8,128)(2,1)S(1)} collective-permute-done((bf16[64,1024]{1,0:T(8,128)(2,1)}, bf16[64,1024]{1,0:T(8,128)(2,1)S(1)}, u32[]{:S(2)}, u32[]{:S(2)}) %collective-permute-start.8) | collective-permute-done | bytes 131104 | tf_op jit(solution)/shard_map/ppermute | solution.py:384
  56.6 5.4 %collective-permute-done.7.refs_1_ = bf16[64,1024]{1,0:T(8,128)(2,1)S(1)} collective-permute-done((bf16[64,1024]{1,0:T(8,128)(2,1)}, bf16[64,1024]{1,0:T(8,128)(2,1)S(1)}, u32[]{:S(2)}, u32[]{:S(2)}) %collective-permute-start.7) | collective-permute-done | bytes 131104 | tf_op jit(solution)/shard_map/ppermute | solution.py:384
  62.9 5.3 %lift.1 = (f32[8,64,512]{2,1,0:T(8,128)S(1)}, bf16[8,64,512]{2,1,0:T(8,128)(2,1)S(1)}) custom-call(s32[4]{0:T(128)S(1)} %pad_add_fusion.info, bf16[64,1024]{1,0:T(8,128)(2,1)S(1)} %copy-done.3, bf16[64,1024]{1,0:T(8,128)(2,1)S(1)} %collective-permute-done.7.refs_1_, bf16[64,1024]{1,0:T(8,128)(2,1)S(1)} %collective-permute-done.8.refs_2_, ...), custom_call_target="tpu_custom_call" | custom-call | flops 1073741824 | bytes 5505024 | tf_op jit(solution)/shard_map/lift/pallas_call | solution.py:209
  68.3 1.9 %collective-permute-done.13 = bf16[8,64,512]{2,1,0:T(8,128)(2,1)S(1)} collective-permute-done((bf16[8,64,512]{2,1,0:T(8,128)(2,1)S(1)}, bf16[8,64,512]{2,1,0:T(8,128)(2,1)S(1)}, u32[]{:S(2)}, u32[]{:S(2)}) %collective-permute-start.13) | collective-permute-done | bytes 524320 | tf_op jit(solution)/shard_map/ppermute | solution.py:387
  71.2 5.8 %all-to-all-start = ((bf16[8,64,512]{2,1,0:T(8,128)(2,1)}), bf16[8,64,512]{2,1,0:T(8,128)(2,1)S(1)}, u32[]{:S(2)}, u32[]{:S(2)}) async-start(bf16[8,64,512]{2,1,0:T(8,128)(2,1)} %add_convert_fusion), calls=%async_computation | async-start | bytes 1048576 | tf_op jit(solution)/shard_map/all_to_all | solution.py:388
  78.2 12.9 %all-to-all-done.parts = bf16[8,64,512]{2,1,0:T(8,128)(2,1)S(1)} async-done(((bf16[8,64,512]{2,1,0:T(8,128)(2,1)}), bf16[8,64,512]{2,1,0:T(8,128)(2,1)S(1)}, u32[]{:S(2)}, u32[]{:S(2)}) %all-to-all-start) | async-done | bytes 524320 | tf_op jit(solution)/shard_map/all_to_all | solution.py:388
  91.2 8.2 %collective-permute-start.14 = (bf16[16,2048]{1,0:T(8,128)(2,1)S(1)}, bf16[16,2048]{1,0:T(8,128)(2,1)S(1)}, u32[]{:S(2)}, u32[]{:S(2)}) collective-permute-start(bf16[16,2048]{1,0:T(8,128)(2,1)S(1)} %get-tuple-element.29), channel_id=1, source_target_pairs={{4,0},{8,4},{12,8},{16,12},{20,16},{24,20},{28,24},{32,28},{36,32}... | collective-permute-start | bytes 196616 | tf_op jit(solution)/shard_map/ppermute | solution.py:392
  99.5 13.9 %denoise_0.1.rest_0_ = bf16[4,16,16,2048]{3,2,1,0:T(8,128)(2,1)} custom-call(s32[4]{0:T(128)S(1)} %copy-done.4, f32[4,16]{1,0:T(4,128)S(1)} %broadcast_divide_fusion.along, f32[4,16]{1,0:T(4,128)S(1)} %get-tuple-element.31.keep, f32[4,16]{1,0:T(4,128)S(1)} %get-tuple-element.30.move, bf16[4,16,16,2048]{3,2,1,0:T(8,128)(2,1)} %latent.5, ...), custom_call_target="tpu_custom_call" | custom-call | flops 2617245696 | bytes 6291456 | tf_op jit(solution)/shard_map/denoise_0/pallas_call | solution.py:317
  113.4 6.5 %denoise_3.1 = bf16[4,16,16,2048]{3,2,1,0:T(8,128)(2,1)} custom-call(s32[4]{0:T(128)S(1)} %copy-done.4, f32[4,16]{1,0:T(4,128)S(1)} %broadcast_divide_fusion.along, f32[4,16]{1,0:T(4,128)S(1)} %get-tuple-element.31.keep, f32[4,16]{1,0:T(4,128)S(1)} %get-tuple-element.30.move, bf16[4,16,16,2048]{3,2,1,0:T(8,128)(2,1)} %latent.5, ...), custom_call_target="tpu_custom_call", output_to_operand_aliasing={{}: (9, {})} | custom-call | flops 872415232 | bytes 2097152 | tf_op jit(solution)/shard_map/denoise_3/pallas_call | solution.py:317
  (37 shorter events, 5.2 us)
Async XLA Ops:
  0.6 29.2 %copy-start = (bf16[2,256,1024]{2,1,0:T(8,128)(2,1)S(1)}, bf16[2,256,1024]{2,1,0:T(8,128)(2,1)}, u32[]{:S(2)}) copy-start(bf16[2,256,1024]{2,1,0:T(8,128)(2,1)} %own.3) | copy-start | bytes 3145732
  0.6 18.9 %collective-permute-start.2 = (bf16[1024,128]{1,0:T(8,128)(2,1)}, bf16[1024,128]{1,0:T(8,128)(2,1)S(1)}, u32[]{:S(2)}, u32[]{:S(2)}) collective-permute-start(bf16[1024,128]{1,0:T(8,128)(2,1)} %param.14), channel_id=1, source_target_pairs={{0,16},{1,65},{16,32},{17,81},{32,48},{33,97},{48,0},{49,113},{64,... | collective-permute-start | bytes 786440 | tf_op jit(solution)/shard_map/ppermute | solution.py:352
  2.3 17.2 %collective-permute-start.4 = (bf16[1024,128]{1,0:T(8,128)(2,1)}, bf16[1024,128]{1,0:T(8,128)(2,1)S(1)}, u32[]{:S(2)}, u32[]{:S(2)}) collective-permute-start(bf16[1024,128]{1,0:T(8,128)(2,1)} %param.14), channel_id=1, source_target_pairs={{0,48},{1,193},{16,0},{17,209},{32,16},{33,225},{48,32},{49,241},{... | collective-permute-start | bytes 786440 | tf_op jit(solution)/shard_map/ppermute | solution.py:352
  4.0 15.6 %collective-permute-start.3 = (bf16[1024,128]{1,0:T(8,128)(2,1)}, bf16[1024,128]{1,0:T(8,128)(2,1)S(1)}, u32[]{:S(2)}, u32[]{:S(2)}) collective-permute-start(bf16[1024,128]{1,0:T(8,128)(2,1)} %param.14), channel_id=1, source_target_pairs={{0,32},{1,129},{16,48},{17,145},{32,0},{33,161},{48,16},{49,177},{... | collective-permute-start | bytes 786440 | tf_op jit(solution)/shard_map/ppermute | solution.py:352
  5.9 14.7 %collective-permute-start.1 = (bf16[64,1024]{1,0:T(8,128)(2,1)}, bf16[64,1024]{1,0:T(8,128)(2,1)S(1)}, u32[]{:S(2)}, u32[]{:S(2)}) collective-permute-start(bf16[64,1024]{1,0:T(8,128)(2,1)} %q.1), channel_id=1, source_target_pairs={{4,0},{8,4},{12,8},{16,12},{20,16},{24,20},{28,24},{32,28},{36,32}... | collective-permute-start | bytes 393224 | tf_op jit(solution)/shard_map/ppermute | solution.py:372
  12.9 12.8 %collective-permute-start = (bf16[64,1024]{1,0:T(8,128)(2,1)}, bf16[64,1024]{1,0:T(8,128)(2,1)S(1)}, u32[]{:S(2)}, u32[]{:S(2)}) collective-permute-start(bf16[64,1024]{1,0:T(8,128)(2,1)} %q.1), channel_id=1, source_target_pairs={{0,4},{4,8},{8,12},{12,16},{16,20},{20,24},{24,28},{28,32},{32,36}... | collective-permute-start | bytes 393224 | tf_op jit(solution)/shard_map/ppermute | solution.py:371
  25.7 36.2 %collective-permute-start.12 = (bf16[4,1024,128]{2,1,0:T(8,128)(2,1)S(1)}, bf16[4,1024,128]{2,1,0:T(8,128)(2,1)S(1)}, u32[]{:S(2)}, u32[]{:S(2)}) collective-permute-start(bf16[4,1024,128]{2,1,0:T(8,128)(2,1)S(1)} %pad_maximum_fusion.refs_4_), channel_id=1, source_target_pairs={{0,192},{1,49},{16,208},{17,1},{32,224},{33,17},{48,240},{49,33},{... | collective-permute-start | bytes 3145736 | tf_op jit(solution)/shard_map/ppermute | solution.py:352
  25.7 36.2 %collective-permute-start.11 = (bf16[4,1024,128]{2,1,0:T(8,128)(2,1)S(1)}, bf16[4,1024,128]{2,1,0:T(8,128)(2,1)}, u32[]{:S(2)}, u32[]{:S(2)}) collective-permute-start(bf16[4,1024,128]{2,1,0:T(8,128)(2,1)S(1)} %pad_maximum_fusion.refs_4_), channel_id=1, source_target_pairs={{0,128},{1,33},{16,144},{17,49},{32,160},{33,1},{48,176},{49,17},{... | collective-permute-start | bytes 3145736 | tf_op jit(solution)/shard_map/ppermute | solution.py:352
  27.8 34.2 %collective-permute-start.10 = (bf16[4,1024,128]{2,1,0:T(8,128)(2,1)S(1)}, bf16[4,1024,128]{2,1,0:T(8,128)(2,1)}, u32[]{:S(2)}, u32[]{:S(2)}) collective-permute-start(bf16[4,1024,128]{2,1,0:T(8,128)(2,1)S(1)} %pad_maximum_fusion.refs_4_), channel_id=1, source_target_pairs={{0,64},{1,17},{16,80},{17,33},{32,96},{33,49},{48,112},{49,1},{64,... | collective-permute-start | bytes 3145736 | tf_op jit(solution)/shard_map/ppermute | solution.py:352
  30.9 13.4 %collective-permute-start.5 = (bf16[64,1152]{1,0:T(8,128)(2,1)S(1)}, bf16[64,1152]{1,0:T(8,128)(2,1)S(1)}, u32[]{:S(2)}, u32[]{:S(2)}) collective-permute-start(bf16[64,1152]{1,0:T(8,128)(2,1)S(1)} %get-tuple-element.21), channel_id=1, source_target_pairs={{0,4},{4,8},{8,12},{12,16},{16,20},{20,24},{24,28},{28,32},{32,36}... | collective-permute-start | bytes 442376 | tf_op jit(solution)/shard_map/ppermute | solution.py:380
  32.8 11.4 %collective-permute-start.6 = (bf16[64,1152]{1,0:T(8,128)(2,1)S(1)}, bf16[64,1152]{1,0:T(8,128)(2,1)S(1)}, u32[]{:S(2)}, u32[]{:S(2)}) collective-permute-start(bf16[64,1152]{1,0:T(8,128)(2,1)S(1)} %get-tuple-element.22), channel_id=1, source_target_pairs={{4,0},{8,4},{12,8},{16,12},{20,16},{24,20},{28,24},{32,28},{36,32}... | collective-permute-start | bytes 442376 | tf_op jit(solution)/shard_map/ppermute | solution.py:379
  44.2 0.7 copy-start.5
  44.3 0.7 copy-start.6
  45.0 33.1 %copy-start.4 = (s32[4]{0:T(128)S(1)}, s32[4]{0:T(128)}, u32[]{:S(2)}) copy-start(s32[4]{0:T(128)} %count.3) | copy-start | bytes 52
  47.2 7.8 %collective-permute-start.9 = (bf16[64,1024]{1,0:T(8,128)(2,1)}, bf16[64,1024]{1,0:T(8,128)(2,1)S(1)}, u32[]{:S(2)}, u32[]{:S(2)}) collective-permute-start(bf16[64,1024]{1,0:T(8,128)(2,1)} %get-tuple-element.24.refs_0_), channel_id=1, source_target_pairs={{0,12},{4,0},{8,4},{12,8},{1,13},{5,1},{9,5},{13,9},{2,14},{6,2},{... | collective-permute-start | bytes 393224 | tf_op jit(solution)/shard_map/ppermute | solution.py:384
  47.7 8.9 %collective-permute-start.8 = (bf16[64,1024]{1,0:T(8,128)(2,1)}, bf16[64,1024]{1,0:T(8,128)(2,1)S(1)}, u32[]{:S(2)}, u32[]{:S(2)}) collective-permute-start(bf16[64,1024]{1,0:T(8,128)(2,1)} %get-tuple-element.24.refs_0_), channel_id=1, source_target_pairs={{0,8},{4,12},{8,0},{12,4},{1,9},{5,13},{9,1},{13,5},{2,10},{6,14},... | collective-permute-start | bytes 393224 | tf_op jit(solution)/shard_map/ppermute | solution.py:384
  55.0 7.0 %collective-permute-start.7 = (bf16[64,1024]{1,0:T(8,128)(2,1)}, bf16[64,1024]{1,0:T(8,128)(2,1)S(1)}, u32[]{:S(2)}, u32[]{:S(2)}) collective-permute-start(bf16[64,1024]{1,0:T(8,128)(2,1)} %get-tuple-element.24.refs_0_), channel_id=1, source_target_pairs={{0,4},{4,8},{8,12},{12,0},{1,5},{5,9},{9,13},{13,1},{2,6},{6,10},{... | collective-permute-start | bytes 393224 | tf_op jit(solution)/shard_map/ppermute | solution.py:384
  55.1 44.4 %copy-start.1 = (bf16[16,128,128]{2,1,0:T(8,128)(2,1)S(1)}, bf16[16,128,128]{2,1,0:T(8,128)(2,1)}, u32[]{:S(2)}) copy-start(bf16[16,128,128]{2,1,0:T(8,128)(2,1)} %qmap.3) | copy-start | bytes 1572868
  55.1 44.4 %copy-start.2 = (bf16[16,128,128]{2,1,0:T(8,128)(2,1)S(1)}, bf16[16,128,128]{2,1,0:T(8,128)(2,1)}, u32[]{:S(2)}) copy-start(bf16[16,128,128]{2,1,0:T(8,128)(2,1)} %kmap.3) | copy-start | bytes 1572868
  62.0 0.9 copy-start.3
  68.2 2.0 %collective-permute-start.13 = (bf16[8,64,512]{2,1,0:T(8,128)(2,1)S(1)}, bf16[8,64,512]{2,1,0:T(8,128)(2,1)S(1)}, u32[]{:S(2)}, u32[]{:S(2)}) collective-permute-start(bf16[8,64,512]{2,1,0:T(8,128)(2,1)S(1)} %get-tuple-element.27), channel_id=1, source_target_pairs={{0,1},{1,0},{2,3},{3,2},{4,5},{5,4},{6,7},{7,6},{8,9},{9,8},{10,11... | collective-permute-start | bytes 1572872 | tf_op jit(solution)/shard_map/ppermute | solution.py:387
  71.2 19.9 %all-to-all-start = ((bf16[8,64,512]{2,1,0:T(8,128)(2,1)}), bf16[8,64,512]{2,1,0:T(8,128)(2,1)S(1)}, u32[]{:S(2)}, u32[]{:S(2)}) async-start(bf16[8,64,512]{2,1,0:T(8,128)(2,1)} %add_convert_fusion), calls=%async_computation | async-start | bytes 1048576 | tf_op jit(solution)/shard_map/all_to_all | solution.py:388
  91.2 22.2 %collective-permute-start.14 = (bf16[16,2048]{1,0:T(8,128)(2,1)S(1)}, bf16[16,2048]{1,0:T(8,128)(2,1)S(1)}, u32[]{:S(2)}, u32[]{:S(2)}) collective-permute-start(bf16[16,2048]{1,0:T(8,128)(2,1)S(1)} %get-tuple-element.29), channel_id=1, source_target_pairs={{4,0},{8,4},{12,8},{16,12},{20,16},{24,20},{28,24},{32,28},{36,32}... | collective-permute-start | bytes 196616 | tf_op jit(solution)/shard_map/ppermute | solution.py:392

commit v3 on v2

--- a/solution.py
+++ b/solution.py
@@ -373,14 +373,16 @@
     line = jnp.stack([lift_weight] + [crossed(lift_weight, d, False) for d in (1, 2, 3)])
 
     edge = jnp.stack([frame > 0, frame < N_FRAME - 1]).astype(jnp.int32)
-    own, stat, latent = own_part(kf_query, kf_kv, cache_kv, kf_latent)
-    q_prev, q_next, line, _ = lax.optimization_barrier((q_prev, q_next, line, own))
+    q_prev, q_next, line = lax.optimization_barrier((q_prev, q_next, line))
     to_prev, to_next = far_parts(q_prev, q_next, cache_kv)
+    query, _ = lax.optimization_barrier((kf_query, to_prev))
+    own, stat, latent = own_part(query, kf_kv, cache_kv, kf_latent)
     after = lax.ppermute(to_prev, FRAME, down)
     before = lax.ppermute(to_next, FRAME, up)
     pieces = [line] + [crossed(line, e, True) for e in (1, 2, 3)]
     updated, moving = join(edge, latent, own, stat, before, after)
 
+    moving, pieces[1] = lax.optimization_barrier((moving, pieces[1]))
     acts = [moving] + [lax.ppermute(moving, "z", ring(4, d)) for d in (1, 2, 3)]
     info = jnp.stack([x, y, z, c]).astype(jnp.int32)
     keep, send = lift(info, acts, pieces)

time: 120 us -> 118 us (0.983)
  waiting for transfers between devices: 36.1 us -> 23.4 us
  starting transfers between devices: 43.5 us -> 52.8 us
  local copies, waits for them, and re-layouts: 1.62 us -> 2.83 us
    ppermute x3, waiting for transfers between devices: 14.2 us -> 6.85 us  [on_device(): acts = [moving] + [lax.ppermute(moving, 'z', ring(4, d)) for d in (1, 2, 3)]]
    ppermute x1, waiting for transfers between devices: 5.09 us -> 0.23 us  [on_device(): q_prev = lax.ppermute(kf_query, FRAME, up)]
    all_to_all x1, starting transfers between devices: 5.77 us -> 8.56 us  [on_device(): parts = lax.all_to_all(parts, ('z', 'h'), 0, 0, tiled=False)]
    ppermute x1, starting transfers between devices: 8.25 us -> 10.5 us  [on_device(): following = lax.ppermute(initial, FRAME, down)]
    ppermute x1, waiting for transfers between devices: 2.04 us -> 0.01 us  [on_device(): before = lax.ppermute(to_next, FRAME, up)]
    ppermute x1, starting transfers between devices: 1.92 us -> 3.82 us  [on_device(): q_prev = lax.ppermute(kf_query, FRAME, up)]
    ppermute x3, starting transfers between devices: 0.47 us -> 2.02 us  [on_device(): acts = [moving] + [lax.ppermute(moving, 'z', ring(4, d)) for d in (1, 2, 3)]]
    ppermute x1, waiting for transfers between devices: 0.01 us -> 1.47 us  [on_device(): q_next = lax.ppermute(kf_query, FRAME, down)]
  transfers between devices with their start and end apart: 16 -> 16, of which waited for: 7 -> 6; matrix products, arithmetic and copies ran while one was open for 2% -> 2% of each run, Pallas kernels for 18% -> 19%
where the time goes in v3:
time: 118 us
  starting transfers between devices  52.8 us (45%)
  Pallas kernels  33.7 us (29%)
  waiting for transfers between devices  23.4 us (20%)
  other arithmetic  2.95 us (2%)
  local copies, waits for them, and re-layouts  2.83 us (2%)
  between operations  1.91 us (2%)
    pallas_call x2, Pallas kernels, denoise(): pl.pallas_call(functools.partial(gap_kernel, first), grid_spec=pltpu.Pref...  20.4 us
    all_to_all x1, waiting for transfers between devices, on_device(): parts = lax.all_to_all(parts, ('z', 'h'), 0, 0, tiled=False)  12.9 us
    ppermute x1, starting transfers between devices, on_device(): following = lax.ppermute(initial, FRAME, down)  10.5 us
    ppermute x1, starting transfers between devices, on_device(): after = lax.ppermute(to_prev, FRAME, down)  9.66 us
    ppermute x6, starting transfers between devices, crossed(): return lax.ppermute(value, ('x', 'y', 'c'), perm)  9.45 us
    all_to_all x1, starting transfers between devices, on_device(): parts = lax.all_to_all(parts, ('z', 'h'), 0, 0, tiled=False)  8.56 us
    ppermute x3, waiting for transfers between devices, on_device(): acts = [moving] + [lax.ppermute(moving, 'z', ring(4, d)) for d in (1, 2, 3)]  6.85 us
    ppermute x1, starting transfers between devices, on_device(): q_next = lax.ppermute(kf_query, FRAME, down)  6.83 us
  transfers between devices with their start and end apart: 16, of which 6 were waited for; matrix products, arithmetic and copies ran while one was open for 2% of the time, Pallas kernels for 19%

profile of v3, /device:TPU:2, one launch (start us, length us, event | category | flops | bytes accessed | tf_op | source)
XLA Modules:
  0.0 117.6 jit_solution(7246304983498179235)
XLA Ops:
  0.6 1.7 %collective-permute-start.2 = (bf16[1024,128]{1,0:T(8,128)(2,1)}, bf16[1024,128]{1,0:T(8,128)(2,1)S(1)}, u32[]{:S(2)}, u32[]{:S(2)}) collective-permute-start(bf16[1024,128]{1,0:T(8,128)(2,1)} %param.14), channel_id=1, source_target_pairs={{0,16},{1,65},{16,32},{17,81},{32,48},{33,97},{48,0},{49,113},{64,... | collective-permute-start | bytes 786440 | tf_op jit(solution)/shard_map/ppermute | solution.py:352
  2.3 1.7 %collective-permute-start.4 = (bf16[1024,128]{1,0:T(8,128)(2,1)}, bf16[1024,128]{1,0:T(8,128)(2,1)S(1)}, u32[]{:S(2)}, u32[]{:S(2)}) collective-permute-start(bf16[1024,128]{1,0:T(8,128)(2,1)} %param.14), channel_id=1, source_target_pairs={{0,48},{1,193},{16,0},{17,209},{32,16},{33,225},{48,32},{49,241},{... | collective-permute-start | bytes 786440 | tf_op jit(solution)/shard_map/ppermute | solution.py:352
  3.9 2.0 %collective-permute-start.3 = (bf16[1024,128]{1,0:T(8,128)(2,1)}, bf16[1024,128]{1,0:T(8,128)(2,1)S(1)}, u32[]{:S(2)}, u32[]{:S(2)}) collective-permute-start(bf16[1024,128]{1,0:T(8,128)(2,1)} %param.14), channel_id=1, source_target_pairs={{0,32},{1,129},{16,48},{17,145},{32,0},{33,161},{48,16},{49,177},{... | collective-permute-start | bytes 786440 | tf_op jit(solution)/shard_map/ppermute | solution.py:352
  5.9 3.8 %collective-permute-start = (bf16[64,1024]{1,0:T(8,128)(2,1)}, bf16[64,1024]{1,0:T(8,128)(2,1)S(1)}, u32[]{:S(2)}, u32[]{:S(2)}) collective-permute-start(bf16[64,1024]{1,0:T(8,128)(2,1)} %q), channel_id=1, source_target_pairs={{0,4},{4,8},{8,12},{12,16},{16,20},{20,24},{24,28},{28,32},{32,36}... | collective-permute-start | bytes 393224 | tf_op jit(solution)/shard_map/ppermute | solution.py:371
  9.8 6.8 %collective-permute-start.1 = (bf16[64,1024]{1,0:T(8,128)(2,1)}, bf16[64,1024]{1,0:T(8,128)(2,1)S(1)}, u32[]{:S(2)}, u32[]{:S(2)}) collective-permute-start(bf16[64,1024]{1,0:T(8,128)(2,1)} %q), channel_id=1, source_target_pairs={{4,0},{8,4},{12,8},{16,12},{20,16},{24,20},{28,24},{32,28},{36,32}... | collective-permute-start | bytes 393224 | tf_op jit(solution)/shard_map/ppermute | solution.py:372
  16.6 1.1 pad_maximum_fusion.refs_4_
  17.9 1.5 %collective-permute-done.1.q_b = bf16[64,1024]{1,0:T(8,128)(2,1)S(1)} collective-permute-done((bf16[64,1024]{1,0:T(8,128)(2,1)}, bf16[64,1024]{1,0:T(8,128)(2,1)S(1)}, u32[]{:S(2)}, u32[]{:S(2)}) %collective-permute-start.1) | collective-permute-done | bytes 131104 | tf_op jit(solution)/shard_map/ppermute | solution.py:372
  19.4 1.5 %collective-permute-start.7 = (bf16[4,1024,128]{2,1,0:T(8,128)(2,1)S(1)}, bf16[4,1024,128]{2,1,0:T(8,128)(2,1)S(1)}, u32[]{:S(2)}, u32[]{:S(2)}) collective-permute-start(bf16[4,1024,128]{2,1,0:T(8,128)(2,1)S(1)} %pad_maximum_fusion.refs_4_), channel_id=1, source_target_pairs={{0,64},{1,17},{16,80},{17,33},{32,96},{33,49},{48,112},{49,1},{64,... | collective-permute-start | bytes 3145736 | tf_op jit(solution)/shard_map/ppermute | solution.py:352
  21.4 2.1 %collective-permute-start.11 = (bf16[4,1024,128]{2,1,0:T(8,128)(2,1)S(1)}, bf16[4,1024,128]{2,1,0:T(8,128)(2,1)}, u32[]{:S(2)}, u32[]{:S(2)}) collective-permute-start(bf16[4,1024,128]{2,1,0:T(8,128)(2,1)S(1)} %pad_maximum_fusion.refs_4_), channel_id=1, source_target_pairs={{0,128},{1,33},{16,144},{17,49},{32,160},{33,1},{48,176},{49,17},{... | collective-permute-start | bytes 3145736 | tf_op jit(solution)/shard_map/ppermute | solution.py:352
  23.6 1.2 %copy-done = bf16[2,256,1024]{2,1,0:T(8,128)(2,1)S(1)} copy-done((bf16[2,256,1024]{2,1,0:T(8,128)(2,1)S(1)}, bf16[2,256,1024]{2,1,0:T(8,128)(2,1)}, u32[]{:S(2)}) %copy-start) | copy-done | bytes 1048600
  25.8 1.9 %collective-permute-start.5 = (bf16[64,1152]{1,0:T(8,128)(2,1)S(1)}, bf16[64,1152]{1,0:T(8,128)(2,1)S(1)}, u32[]{:S(2)}, u32[]{:S(2)}) collective-permute-start(bf16[64,1152]{1,0:T(8,128)(2,1)S(1)} %get-tuple-element.26), channel_id=1, source_target_pairs={{0,4},{4,8},{8,12},{12,16},{16,20},{20,24},{24,28},{28,32},{32,36}... | collective-permute-start | bytes 442376 | tf_op jit(solution)/shard_map/ppermute | solution.py:381
  27.7 9.7 %collective-permute-start.6 = (bf16[64,1152]{1,0:T(8,128)(2,1)S(1)}, bf16[64,1152]{1,0:T(8,128)(2,1)S(1)}, u32[]{:S(2)}, u32[]{:S(2)}) collective-permute-start(bf16[64,1152]{1,0:T(8,128)(2,1)S(1)} %get-tuple-element.21), channel_id=1, source_target_pairs={{4,0},{8,4},{12,8},{16,12},{20,16},{24,20},{28,24},{32,28},{36,32}... | collective-permute-start | bytes 442376 | tf_op jit(solution)/shard_map/ppermute | solution.py:380
  38.1 4.7 %own_part.1 = (f32[64,1024]{1,0:T(8,128)}, f32[64,128]{1,0:T(8,128)}, bf16[64,1024]{1,0:T(8,128)(2,1)}) custom-call(bf16[64,1024]{1,0:T(8,128)(2,1)} %q, bf16[2,64,1024]{2,1,0:T(8,128)(2,1)} %kv.1, bf16[2,256,1024]{2,1,0:T(8,128)(2,1)} %own.3, bf16[64,1024]{1,0:T(8,128)(2,1)} %latent.3), custom_call_target="tpu_custom_call" | custom-call | flops 83886080 | bytes 1703936 | tf_op jit(solution)/shard_map/own_part/pallas_call | solution.py:68
  43.4 2.2 %join.1 = (bf16[64,1024]{1,0:T(8,128)(2,1)}, bf16[64,1024]{1,0:T(8,128)(2,1)}) custom-call(s32[2]{0:T(128)} %add_convert_fusion.1.edge, bf16[64,1024]{1,0:T(8,128)(2,1)} %get-tuple-element.23.latent, f32[64,1024]{1,0:T(8,128)} %get-tuple-element.24.own, f32[64,128]{1,0:T(8,128)} %get-tuple-element.25.stat, bf16[64,1152]{1,0:T(8,128)(2,1)} %copy-done.5, ...), custom_call_target="tpu_custom_call" | custom-call | flops 524288 | bytes 786432 | tf_op jit(solution)/shard_map/join/pallas_call | solution.py:159
  45.8 1.9 %collective-permute-start.8 = (bf16[64,1024]{1,0:T(8,128)(2,1)}, bf16[64,1024]{1,0:T(8,128)(2,1)S(1)}, u32[]{:S(2)}, u32[]{:S(2)}) collective-permute-start(bf16[64,1024]{1,0:T(8,128)(2,1)} %get-tuple-element.30.refs_0_), channel_id=1, source_target_pairs={{0,4},{4,8},{8,12},{12,0},{1,5},{5,9},{9,13},{13,1},{2,6},{6,10},{... | collective-permute-start | bytes 393224 | tf_op jit(solution)/shard_map/ppermute | solution.py:386
  47.8 5.1 %collective-permute-done.10.refs_3_ = bf16[64,1024]{1,0:T(8,128)(2,1)S(1)} collective-permute-done((bf16[64,1024]{1,0:T(8,128)(2,1)}, bf16[64,1024]{1,0:T(8,128)(2,1)S(1)}, u32[]{:S(2)}, u32[]{:S(2)}) %collective-permute-start.10) | collective-permute-done | bytes 131104 | tf_op jit(solution)/shard_map/ppermute | solution.py:386
  52.9 1.7 %collective-permute-done.8.refs_1_ = bf16[64,1024]{1,0:T(8,128)(2,1)S(1)} collective-permute-done((bf16[64,1024]{1,0:T(8,128)(2,1)}, bf16[64,1024]{1,0:T(8,128)(2,1)S(1)}, u32[]{:S(2)}, u32[]{:S(2)}) %collective-permute-start.8) | collective-permute-done | bytes 131104 | tf_op jit(solution)/shard_map/ppermute | solution.py:386
  55.6 5.3 %lift.1 = (f32[8,64,512]{2,1,0:T(8,128)S(1)}, bf16[8,64,512]{2,1,0:T(8,128)(2,1)S(1)}) custom-call(s32[4]{0:T(128)S(1)} %pad_add_fusion.info, bf16[64,1024]{1,0:T(8,128)(2,1)S(1)} %copy-done.3, bf16[64,1024]{1,0:T(8,128)(2,1)S(1)} %collective-permute-done.8.refs_1_, bf16[64,1024]{1,0:T(8,128)(2,1)S(1)} %collective-permute-done.9.refs_2_, ...), custom_call_target="tpu_custom_call" | custom-call | flops 1073741824 | bytes 5505024 | tf_op jit(solution)/shard_map/lift/pallas_call | solution.py:209
  61.0 1.9 %collective-permute-done.13 = bf16[8,64,512]{2,1,0:T(8,128)(2,1)S(1)} collective-permute-done((bf16[8,64,512]{2,1,0:T(8,128)(2,1)S(1)}, bf16[8,64,512]{2,1,0:T(8,128)(2,1)S(1)}, u32[]{:S(2)}, u32[]{:S(2)}) %collective-permute-start.13) | collective-permute-done | bytes 524320 | tf_op jit(solution)/shard_map/ppermute | solution.py:389
  63.9 8.6 %all-to-all-start = ((bf16[8,64,512]{2,1,0:T(8,128)(2,1)}), bf16[8,64,512]{2,1,0:T(8,128)(2,1)S(1)}, u32[]{:S(2)}, u32[]{:S(2)}) async-start(bf16[8,64,512]{2,1,0:T(8,128)(2,1)} %add_convert_fusion), calls=%async_computation | async-start | bytes 1048576 | tf_op jit(solution)/shard_map/all_to_all | solution.py:390
  73.7 12.9 %all-to-all-done.parts = bf16[8,64,512]{2,1,0:T(8,128)(2,1)S(1)} async-done(((bf16[8,64,512]{2,1,0:T(8,128)(2,1)}), bf16[8,64,512]{2,1,0:T(8,128)(2,1)S(1)}, u32[]{:S(2)}, u32[]{:S(2)}) %all-to-all-start) | async-done | bytes 524320 | tf_op jit(solution)/shard_map/all_to_all | solution.py:390
  86.6 10.5 %collective-permute-start.14 = (bf16[16,2048]{1,0:T(8,128)(2,1)S(1)}, bf16[16,2048]{1,0:T(8,128)(2,1)S(1)}, u32[]{:S(2)}, u32[]{:S(2)}) collective-permute-start(bf16[16,2048]{1,0:T(8,128)(2,1)S(1)} %get-tuple-element.35), channel_id=1, source_target_pairs={{4,0},{8,4},{12,8},{16,12},{20,16},{24,20},{28,24},{32,28},{36,32}... | collective-permute-start | bytes 196616 | tf_op jit(solution)/shard_map/ppermute | solution.py:394
  97.2 13.9 %denoise_0.1.rest_0_ = bf16[4,16,16,2048]{3,2,1,0:T(8,128)(2,1)} custom-call(s32[4]{0:T(128)S(1)} %copy-done.4, f32[4,16]{1,0:T(4,128)S(1)} %broadcast_divide_fusion.along, f32[4,16]{1,0:T(4,128)S(1)} %get-tuple-element.37.keep, f32[4,16]{1,0:T(4,128)S(1)} %get-tuple-element.36.move, bf16[4,16,16,2048]{3,2,1,0:T(8,128)(2,1)} %latent.5, ...), custom_call_target="tpu_custom_call" | custom-call | flops 2617245696 | bytes 6291456 | tf_op jit(solution)/shard_map/denoise_0/pallas_call | solution.py:317
  111.1 6.5 %denoise_3.1 = bf16[4,16,16,2048]{3,2,1,0:T(8,128)(2,1)} custom-call(s32[4]{0:T(128)S(1)} %copy-done.4, f32[4,16]{1,0:T(4,128)S(1)} %broadcast_divide_fusion.along, f32[4,16]{1,0:T(4,128)S(1)} %get-tuple-element.37.keep, f32[4,16]{1,0:T(4,128)S(1)} %get-tuple-element.36.move, bf16[4,16,16,2048]{3,2,1,0:T(8,128)(2,1)} %latent.5, ...), custom_call_target="tpu_custom_call", output_to_operand_aliasing={{}: (9, {})} | custom-call | flops 872415232 | bytes 2097152 | tf_op jit(solution)/shard_map/denoise_3/pallas_call | solution.py:317
  (37 shorter events, 5.5 us)
Async XLA Ops:
  0.6 16.0 %collective-permute-start.2 = (bf16[1024,128]{1,0:T(8,128)(2,1)}, bf16[1024,128]{1,0:T(8,128)(2,1)S(1)}, u32[]{:S(2)}, u32[]{:S(2)}) collective-permute-start(bf16[1024,128]{1,0:T(8,128)(2,1)} %param.14), channel_id=1, source_target_pairs={{0,16},{1,65},{16,32},{17,81},{32,48},{33,97},{48,0},{49,113},{64,... | collective-permute-start | bytes 786440 | tf_op jit(solution)/shard_map/ppermute | solution.py:352
  2.3 14.3 %collective-permute-start.4 = (bf16[1024,128]{1,0:T(8,128)(2,1)}, bf16[1024,128]{1,0:T(8,128)(2,1)S(1)}, u32[]{:S(2)}, u32[]{:S(2)}) collective-permute-start(bf16[1024,128]{1,0:T(8,128)(2,1)} %param.14), channel_id=1, source_target_pairs={{0,48},{1,193},{16,0},{17,209},{32,16},{33,225},{48,32},{49,241},{... | collective-permute-start | bytes 786440 | tf_op jit(solution)/shard_map/ppermute | solution.py:352
  3.9 12.7 %collective-permute-start.3 = (bf16[1024,128]{1,0:T(8,128)(2,1)}, bf16[1024,128]{1,0:T(8,128)(2,1)S(1)}, u32[]{:S(2)}, u32[]{:S(2)}) collective-permute-start(bf16[1024,128]{1,0:T(8,128)(2,1)} %param.14), channel_id=1, source_target_pairs={{0,32},{1,129},{16,48},{17,145},{32,0},{33,161},{48,16},{49,177},{... | collective-permute-start | bytes 786440 | tf_op jit(solution)/shard_map/ppermute | solution.py:352
  5.9 12.0 %collective-permute-start = (bf16[64,1024]{1,0:T(8,128)(2,1)}, bf16[64,1024]{1,0:T(8,128)(2,1)S(1)}, u32[]{:S(2)}, u32[]{:S(2)}) collective-permute-start(bf16[64,1024]{1,0:T(8,128)(2,1)} %q), channel_id=1, source_target_pairs={{0,4},{4,8},{8,12},{12,16},{16,20},{20,24},{24,28},{28,32},{32,36}... | collective-permute-start | bytes 393224 | tf_op jit(solution)/shard_map/ppermute | solution.py:371
  9.8 9.6 %collective-permute-start.1 = (bf16[64,1024]{1,0:T(8,128)(2,1)}, bf16[64,1024]{1,0:T(8,128)(2,1)S(1)}, u32[]{:S(2)}, u32[]{:S(2)}) collective-permute-start(bf16[64,1024]{1,0:T(8,128)(2,1)} %q), channel_id=1, source_target_pairs={{4,0},{8,4},{12,8},{16,12},{20,16},{24,20},{28,24},{32,28},{36,32}... | collective-permute-start | bytes 393224 | tf_op jit(solution)/shard_map/ppermute | solution.py:372
  19.4 26.3 %collective-permute-start.7 = (bf16[4,1024,128]{2,1,0:T(8,128)(2,1)S(1)}, bf16[4,1024,128]{2,1,0:T(8,128)(2,1)S(1)}, u32[]{:S(2)}, u32[]{:S(2)}) collective-permute-start(bf16[4,1024,128]{2,1,0:T(8,128)(2,1)S(1)} %pad_maximum_fusion.refs_4_), channel_id=1, source_target_pairs={{0,64},{1,17},{16,80},{17,33},{32,96},{33,49},{48,112},{49,1},{64,... | collective-permute-start | bytes 3145736 | tf_op jit(solution)/shard_map/ppermute | solution.py:352
  20.9 26.9 %collective-permute-start.12 = (bf16[4,1024,128]{2,1,0:T(8,128)(2,1)S(1)}, bf16[4,1024,128]{2,1,0:T(8,128)(2,1)}, u32[]{:S(2)}, u32[]{:S(2)}) collective-permute-start(bf16[4,1024,128]{2,1,0:T(8,128)(2,1)S(1)} %pad_maximum_fusion.refs_4_), channel_id=1, source_target_pairs={{0,192},{1,49},{16,208},{17,1},{32,224},{33,17},{48,240},{49,33},{... | collective-permute-start | bytes 3145736 | tf_op jit(solution)/shard_map/ppermute | solution.py:352
  21.4 26.4 %collective-permute-start.11 = (bf16[4,1024,128]{2,1,0:T(8,128)(2,1)S(1)}, bf16[4,1024,128]{2,1,0:T(8,128)(2,1)}, u32[]{:S(2)}, u32[]{:S(2)}) collective-permute-start(bf16[4,1024,128]{2,1,0:T(8,128)(2,1)S(1)} %pad_maximum_fusion.refs_4_), channel_id=1, source_target_pairs={{0,128},{1,33},{16,144},{17,49},{32,160},{33,1},{48,176},{49,17},{... | collective-permute-start | bytes 3145736 | tf_op jit(solution)/shard_map/ppermute | solution.py:352
  23.6 1.2 %copy-start = (bf16[2,256,1024]{2,1,0:T(8,128)(2,1)S(1)}, bf16[2,256,1024]{2,1,0:T(8,128)(2,1)}, u32[]{:S(2)}) copy-start(bf16[2,256,1024]{2,1,0:T(8,128)(2,1)} %own.3) | copy-start | bytes 3145732
  25.8 16.9 %collective-permute-start.5 = (bf16[64,1152]{1,0:T(8,128)(2,1)S(1)}, bf16[64,1152]{1,0:T(8,128)(2,1)S(1)}, u32[]{:S(2)}, u32[]{:S(2)}) collective-permute-start(bf16[64,1152]{1,0:T(8,128)(2,1)S(1)} %get-tuple-element.26), channel_id=1, source_target_pairs={{0,4},{4,8},{8,12},{12,16},{16,20},{20,24},{24,28},{28,32},{32,36}... | collective-permute-start | bytes 442376 | tf_op jit(solution)/shard_map/ppermute | solution.py:381
  27.7 15.0 %collective-permute-start.6 = (bf16[64,1152]{1,0:T(8,128)(2,1)S(1)}, bf16[64,1152]{1,0:T(8,128)(2,1)S(1)}, u32[]{:S(2)}, u32[]{:S(2)}) collective-permute-start(bf16[64,1152]{1,0:T(8,128)(2,1)S(1)} %get-tuple-element.21), channel_id=1, source_target_pairs={{4,0},{8,4},{12,8},{16,12},{20,16},{24,20},{28,24},{32,28},{36,32}... | collective-permute-start | bytes 442376 | tf_op jit(solution)/shard_map/ppermute | solution.py:380
  42.7 0.7 copy-start.5
  42.7 0.7 copy-start.6
  43.4 30.1 %copy-start.4 = (s32[4]{0:T(128)S(1)}, s32[4]{0:T(128)}, u32[]{:S(2)}) copy-start(s32[4]{0:T(128)} %count.3) | copy-start | bytes 52
  45.7 7.3 %collective-permute-start.10 = (bf16[64,1024]{1,0:T(8,128)(2,1)}, bf16[64,1024]{1,0:T(8,128)(2,1)S(1)}, u32[]{:S(2)}, u32[]{:S(2)}) collective-permute-start(bf16[64,1024]{1,0:T(8,128)(2,1)} %get-tuple-element.30.refs_0_), channel_id=1, source_target_pairs={{0,12},{4,0},{8,4},{12,8},{1,13},{5,1},{9,5},{13,9},{2,14},{6,2},{... | collective-permute-start | bytes 393224 | tf_op jit(solution)/shard_map/ppermute | solution.py:386
  45.7 7.3 %collective-permute-start.9 = (bf16[64,1024]{1,0:T(8,128)(2,1)}, bf16[64,1024]{1,0:T(8,128)(2,1)S(1)}, u32[]{:S(2)}, u32[]{:S(2)}) collective-permute-start(bf16[64,1024]{1,0:T(8,128)(2,1)} %get-tuple-element.30.refs_0_), channel_id=1, source_target_pairs={{0,8},{4,12},{8,0},{12,4},{1,9},{5,13},{9,1},{13,5},{2,10},{6,14},... | collective-permute-start | bytes 393224 | tf_op jit(solution)/shard_map/ppermute | solution.py:386
  45.8 8.9 %collective-permute-start.8 = (bf16[64,1024]{1,0:T(8,128)(2,1)}, bf16[64,1024]{1,0:T(8,128)(2,1)S(1)}, u32[]{:S(2)}, u32[]{:S(2)}) collective-permute-start(bf16[64,1024]{1,0:T(8,128)(2,1)} %get-tuple-element.30.refs_0_), channel_id=1, source_target_pairs={{0,4},{4,8},{8,12},{12,0},{1,5},{5,9},{9,13},{13,1},{2,6},{6,10},{... | collective-permute-start | bytes 393224 | tf_op jit(solution)/shard_map/ppermute | solution.py:386
  47.8 49.4 %copy-start.1 = (bf16[16,128,128]{2,1,0:T(8,128)(2,1)S(1)}, bf16[16,128,128]{2,1,0:T(8,128)(2,1)}, u32[]{:S(2)}) copy-start(bf16[16,128,128]{2,1,0:T(8,128)(2,1)} %qmap.3) | copy-start | bytes 1572868
  47.8 49.4 %copy-start.2 = (bf16[16,128,128]{2,1,0:T(8,128)(2,1)S(1)}, bf16[16,128,128]{2,1,0:T(8,128)(2,1)}, u32[]{:S(2)}) copy-start(bf16[16,128,128]{2,1,0:T(8,128)(2,1)} %kmap.3) | copy-start | bytes 1572868
  54.7 0.9 copy-start.3
  60.9 2.0 %collective-permute-start.13 = (bf16[8,64,512]{2,1,0:T(8,128)(2,1)S(1)}, bf16[8,64,512]{2,1,0:T(8,128)(2,1)S(1)}, u32[]{:S(2)}, u32[]{:S(2)}) collective-permute-start(bf16[8,64,512]{2,1,0:T(8,128)(2,1)S(1)} %get-tuple-element.33), channel_id=1, source_target_pairs={{0,1},{1,0},{2,3},{3,2},{4,5},{5,4},{6,7},{7,6},{8,9},{9,8},{10,11... | collective-permute-start | bytes 1572872 | tf_op jit(solution)/shard_map/ppermute | solution.py:389
  63.9 22.7 %all-to-all-start = ((bf16[8,64,512]{2,1,0:T(8,128)(2,1)}), bf16[8,64,512]{2,1,0:T(8,128)(2,1)S(1)}, u32[]{:S(2)}, u32[]{:S(2)}) async-start(bf16[8,64,512]{2,1,0:T(8,128)(2,1)} %add_convert_fusion), calls=%async_computation | async-start | bytes 1048576 | tf_op jit(solution)/shard_map/all_to_all | solution.py:390
  86.6 24.4 %collective-permute-start.14 = (bf16[16,2048]{1,0:T(8,128)(2,1)S(1)}, bf16[16,2048]{1,0:T(8,128)(2,1)S(1)}, u32[]{:S(2)}, u32[]{:S(2)}) collective-permute-start(bf16[16,2048]{1,0:T(8,128)(2,1)S(1)} %get-tuple-element.35), channel_id=1, source_target_pairs={{4,0},{8,4},{12,8},{16,12},{20,16},{24,20},{28,24},{32,28},{36,32}... | collective-permute-start | bytes 196616 | tf_op jit(solution)/shard_map/ppermute | solution.py:394

commit v4 on v3

--- a/solution.py
+++ b/solution.py
@@ -214,7 +214,7 @@
             jax.ShapeDtypeStruct((8, rows, 4 * HD), BF),
         ),
         scratch_shapes=[pltpu.VMEM((4 * rows, width), BF)],
-        compiler_params=pltpu.CompilerParams(vmem_limit_bytes=24 << 20),
+        compiler_params=pltpu.CompilerParams(vmem_limit_bytes=56 << 20),
         cost_estimate=pl.CostEstimate(
             flops=2 * 4 * rows * width * 16 * HD,
             bytes_accessed=2 * (16 * width * HD + 4 * rows * width + 48 * rows * HD),

time: 118 us -> 122 us (1.034)
  Pallas kernels: 33.7 us -> 35.7 us
  other arithmetic: 2.95 us -> 4.66 us
    pallas_call x1, Pallas kernels: 5.31 us -> 7.32 us  [lift(): pl.pallas_call(lift_kernel, in_specs=[pl.BlockSpec(memory_space=pltpu.SME...]
    unnamed x14 -> x22, local copies, waits for them, and re-layouts: 2.83 us -> 2.61 us
  transfers between devices with their start and end apart: 16 -> 16, of which waited for: 6 -> 6; matrix products, arithmetic and copies ran while one was open for 2% -> 2% of each run, Pallas kernels for 19% -> 18%
where the time goes in v4:
time: 122 us; the launch traced here: 121 us
  starting transfers between devices  53.4 us (44%)
  Pallas kernels  35.7 us (29%)
  waiting for transfers between devices  23 us (19%)
  other arithmetic  4.66 us (4%)
  local copies, waits for them, and re-layouts  2.61 us (2%)
  between operations  1.91 us (2%)
    pallas_call x2, Pallas kernels, denoise(): pl.pallas_call(functools.partial(gap_kernel, first), grid_spec=pltpu.Pref...  20.4 us
    all_to_all x1, waiting for transfers between devices, on_device(): parts = lax.all_to_all(parts, ('z', 'h'), 0, 0, tiled=False)  12.9 us
    ppermute x1, starting transfers between devices, on_device(): following = lax.ppermute(initial, FRAME, down)  11.1 us
    ppermute x1, starting transfers between devices, on_device(): after = lax.ppermute(to_prev, FRAME, down)  9.66 us
    ppermute x6, starting transfers between devices, crossed(): return lax.ppermute(value, ('x', 'y', 'c'), perm)  9.45 us
    all_to_all x1, starting transfers between devices, on_device(): parts = lax.all_to_all(parts, ('z', 'h'), 0, 0, tiled=False)  8.55 us
    pallas_call x1, Pallas kernels, lift(): pl.pallas_call(lift_kernel, in_specs=[pl.BlockSpec(memory_space=pltpu.SME...  7.32 us
    ppermute x1, starting transfers between devices, on_device(): q_next = lax.ppermute(kf_query, FRAME, down)  6.83 us
  transfers between devices with their start and end apart: 16, of which 6 were waited for; matrix products, arithmetic and copies ran while one was open for 2% of the time, Pallas kernels for 18%

profile of v4, /device:TPU:2, one launch (start us, length us, event | category | flops | bytes accessed | tf_op | source)
XLA Modules:
  0.0 121.3 jit_solution(12546741489068057558)
XLA Ops:
  0.6 1.7 %collective-permute-start.2 = (bf16[1024,128]{1,0:T(8,128)(2,1)}, bf16[1024,128]{1,0:T(8,128)(2,1)S(1)}, u32[]{:S(2)}, u32[]{:S(2)}) collective-permute-start(bf16[1024,128]{1,0:T(8,128)(2,1)} %param.14), channel_id=1, source_target_pairs={{0,16},{1,65},{16,32},{17,81},{32,48},{33,97},{48,0},{49,113},{64,... | collective-permute-start | bytes 786440 | tf_op jit(solution)/shard_map/ppermute | solution.py:352
  2.3 1.7 %collective-permute-start.4 = (bf16[1024,128]{1,0:T(8,128)(2,1)}, bf16[1024,128]{1,0:T(8,128)(2,1)S(1)}, u32[]{:S(2)}, u32[]{:S(2)}) collective-permute-start(bf16[1024,128]{1,0:T(8,128)(2,1)} %param.14), channel_id=1, source_target_pairs={{0,48},{1,193},{16,0},{17,209},{32,16},{33,225},{48,32},{49,241},{... | collective-permute-start | bytes 786440 | tf_op jit(solution)/shard_map/ppermute | solution.py:352
  3.9 2.0 %collective-permute-start.3 = (bf16[1024,128]{1,0:T(8,128)(2,1)}, bf16[1024,128]{1,0:T(8,128)(2,1)S(1)}, u32[]{:S(2)}, u32[]{:S(2)}) collective-permute-start(bf16[1024,128]{1,0:T(8,128)(2,1)} %param.14), channel_id=1, source_target_pairs={{0,32},{1,129},{16,48},{17,145},{32,0},{33,161},{48,16},{49,177},{... | collective-permute-start | bytes 786440 | tf_op jit(solution)/shard_map/ppermute | solution.py:352
  5.9 3.8 %collective-permute-start = (bf16[64,1024]{1,0:T(8,128)(2,1)}, bf16[64,1024]{1,0:T(8,128)(2,1)S(1)}, u32[]{:S(2)}, u32[]{:S(2)}) collective-permute-start(bf16[64,1024]{1,0:T(8,128)(2,1)} %q), channel_id=1, source_target_pairs={{0,4},{4,8},{8,12},{12,16},{16,20},{20,24},{24,28},{28,32},{32,36}... | collective-permute-start | bytes 393224 | tf_op jit(solution)/shard_map/ppermute | solution.py:371
  9.8 6.8 %collective-permute-start.1 = (bf16[64,1024]{1,0:T(8,128)(2,1)}, bf16[64,1024]{1,0:T(8,128)(2,1)S(1)}, u32[]{:S(2)}, u32[]{:S(2)}) collective-permute-start(bf16[64,1024]{1,0:T(8,128)(2,1)} %q), channel_id=1, source_target_pairs={{4,0},{8,4},{12,8},{16,12},{20,16},{24,20},{28,24},{32,28},{36,32}... | collective-permute-start | bytes 393224 | tf_op jit(solution)/shard_map/ppermute | solution.py:372
  17.9 1.5 %collective-permute-done.1.q_b = bf16[64,1024]{1,0:T(8,128)(2,1)S(1)} collective-permute-done((bf16[64,1024]{1,0:T(8,128)(2,1)}, bf16[64,1024]{1,0:T(8,128)(2,1)S(1)}, u32[]{:S(2)}, u32[]{:S(2)}) %collective-permute-start.1) | collective-permute-done | bytes 131104 | tf_op jit(solution)/shard_map/ppermute | solution.py:372
  19.4 1.5 %collective-permute-start.7 = (bf16[4,1024,128]{2,1,0:T(8,128)(2,1)S(1)}, bf16[4,1024,128]{2,1,0:T(8,128)(2,1)S(1)}, u32[]{:S(2)}, u32[]{:S(2)}) collective-permute-start(bf16[4,1024,128]{2,1,0:T(8,128)(2,1)S(1)} %pad_maximum_fusion.refs_4_), channel_id=1, source_target_pairs={{0,64},{1,17},{16,80},{17,33},{32,96},{33,49},{48,112},{49,1},{64,... | collective-permute-start | bytes 3145736 | tf_op jit(solution)/shard_map/ppermute | solution.py:352
  21.4 2.1 %collective-permute-start.11 = (bf16[4,1024,128]{2,1,0:T(8,128)(2,1)S(1)}, bf16[4,1024,128]{2,1,0:T(8,128)(2,1)}, u32[]{:S(2)}, u32[]{:S(2)}) collective-permute-start(bf16[4,1024,128]{2,1,0:T(8,128)(2,1)S(1)} %pad_maximum_fusion.refs_4_), channel_id=1, source_target_pairs={{0,128},{1,33},{16,144},{17,49},{32,160},{33,1},{48,176},{49,17},{... | collective-permute-start | bytes 3145736 | tf_op jit(solution)/shard_map/ppermute | solution.py:352
  23.6 1.2 %copy-done = bf16[2,256,1024]{2,1,0:T(8,128)(2,1)S(1)} copy-done((bf16[2,256,1024]{2,1,0:T(8,128)(2,1)S(1)}, bf16[2,256,1024]{2,1,0:T(8,128)(2,1)}, u32[]{:S(2)}) %copy-start) | copy-done | bytes 1048600
  25.8 1.9 %collective-permute-start.5 = (bf16[64,1152]{1,0:T(8,128)(2,1)S(1)}, bf16[64,1152]{1,0:T(8,128)(2,1)S(1)}, u32[]{:S(2)}, u32[]{:S(2)}) collective-permute-start(bf16[64,1152]{1,0:T(8,128)(2,1)S(1)} %get-tuple-element.26), channel_id=1, source_target_pairs={{0,4},{4,8},{8,12},{12,16},{16,20},{20,24},{24,28},{28,32},{32,36}... | collective-permute-start | bytes 442376 | tf_op jit(solution)/shard_map/ppermute | solution.py:381
  27.7 9.7 %collective-permute-start.6 = (bf16[64,1152]{1,0:T(8,128)(2,1)S(1)}, bf16[64,1152]{1,0:T(8,128)(2,1)S(1)}, u32[]{:S(2)}, u32[]{:S(2)}) collective-permute-start(bf16[64,1152]{1,0:T(8,128)(2,1)S(1)} %get-tuple-element.21), channel_id=1, source_target_pairs={{4,0},{8,4},{12,8},{16,12},{20,16},{24,20},{28,24},{32,28},{36,32}... | collective-permute-start | bytes 442376 | tf_op jit(solution)/shard_map/ppermute | solution.py:380
  38.0 4.7 %own_part.1 = (f32[64,1024]{1,0:T(8,128)}, f32[64,128]{1,0:T(8,128)}, bf16[64,1024]{1,0:T(8,128)(2,1)}) custom-call(bf16[64,1024]{1,0:T(8,128)(2,1)} %q, bf16[2,64,1024]{2,1,0:T(8,128)(2,1)} %kv.1, bf16[2,256,1024]{2,1,0:T(8,128)(2,1)} %own.3, bf16[64,1024]{1,0:T(8,128)(2,1)} %latent.3), custom_call_target="tpu_custom_call" | custom-call | flops 83886080 | bytes 1703936 | tf_op jit(solution)/shard_map/own_part/pallas_call | solution.py:68
  43.4 2.2 %join.1 = (bf16[64,1024]{1,0:T(8,128)(2,1)}, bf16[64,1024]{1,0:T(8,128)(2,1)}) custom-call(s32[2]{0:T(128)} %add_convert_fusion.1.edge, bf16[64,1024]{1,0:T(8,128)(2,1)} %get-tuple-element.23.latent, f32[64,1024]{1,0:T(8,128)} %get-tuple-element.24.own, f32[64,128]{1,0:T(8,128)} %get-tuple-element.25.stat, bf16[64,1152]{1,0:T(8,128)(2,1)} %copy-done.6, ...), custom_call_target="tpu_custom_call" | custom-call | flops 524288 | bytes 786432 | tf_op jit(solution)/shard_map/join/pallas_call | solution.py:159
  45.9 1.9 %collective-permute-start.8 = (bf16[64,1024]{1,0:T(8,128)(2,1)}, bf16[64,1024]{1,0:T(8,128)(2,1)S(1)}, u32[]{:S(2)}, u32[]{:S(2)}) collective-permute-start(bf16[64,1024]{1,0:T(8,128)(2,1)} %get-tuple-element.30.refs_0_), channel_id=1, source_target_pairs={{0,4},{4,8},{8,12},{12,0},{1,5},{5,9},{9,13},{13,1},{2,6},{6,10},{... | collective-permute-start | bytes 393224 | tf_op jit(solution)/shard_map/ppermute | solution.py:386
  48.4 4.6 %collective-permute-done.10.refs_3_ = bf16[64,1024]{1,0:T(8,128)(2,1)S(1)} collective-permute-done((bf16[64,1024]{1,0:T(8,128)(2,1)}, bf16[64,1024]{1,0:T(8,128)(2,1)S(1)}, u32[]{:S(2)}, u32[]{:S(2)}) %collective-permute-start.10) | collective-permute-done | bytes 131104 | tf_op jit(solution)/shard_map/ppermute | solution.py:386
  53.0 1.7 %collective-permute-done.8.refs_1_ = bf16[64,1024]{1,0:T(8,128)(2,1)S(1)} collective-permute-done((bf16[64,1024]{1,0:T(8,128)(2,1)}, bf16[64,1024]{1,0:T(8,128)(2,1)S(1)}, u32[]{:S(2)}, u32[]{:S(2)}) %collective-permute-start.8) | collective-permute-done | bytes 131104 | tf_op jit(solution)/shard_map/ppermute | solution.py:386
  55.4 7.3 %lift.1 = (f32[8,64,512]{2,1,0:T(8,128)}, bf16[8,64,512]{2,1,0:T(8,128)(2,1)}) custom-call(s32[4]{0:T(128)} %pad_add_fusion.info, bf16[64,1024]{1,0:T(8,128)(2,1)} %get-tuple-element.30.refs_0_, bf16[64,1024]{1,0:T(8,128)(2,1)} %copy-done.10, bf16[64,1024]{1,0:T(8,128)(2,1)} %copy-done.9, bf16[64,1024]{1,0:T(8,128)(2,1)} %copy-done.8, ...), custom_call_target="tpu_custom_call" | custom-call | flops 1073741824 | bytes 5505024 | tf_op jit(solution)/shard_map/lift/pallas_call | solution.py:209
  62.7 2.1 %collective-permute-done.13 = bf16[8,64,512]{2,1,0:T(8,128)(2,1)S(1)} collective-permute-done((bf16[8,64,512]{2,1,0:T(8,128)(2,1)}, bf16[8,64,512]{2,1,0:T(8,128)(2,1)S(1)}, u32[]{:S(2)}, u32[]{:S(2)}) %collective-permute-start.13) | collective-permute-done | bytes 524320 | tf_op jit(solution)/shard_map/ppermute | solution.py:389
  64.8 2.2 %add_convert_fusion = bf16[8,64,512]{2,1,0:T(8,128)(2,1)} fusion(f32[8,64,512]{2,1,0:T(8,128)} %get-tuple-element.32, bf16[8,64,512]{2,1,0:T(8,128)(2,1)S(1)} %collective-permute-done.13), kind=kLoop, calls=%fused_computation.1 | loop fusion | flops 786432 | bytes 2097152 | tf_op jit(solution)/shard_map/convert_element_type | solution.py:389
  67.0 8.6 %all-to-all-start = ((bf16[8,64,512]{2,1,0:T(8,128)(2,1)}), bf16[8,64,512]{2,1,0:T(8,128)(2,1)S(1)}, u32[]{:S(2)}, u32[]{:S(2)}) async-start(bf16[8,64,512]{2,1,0:T(8,128)(2,1)} %add_convert_fusion), calls=%async_computation | async-start | bytes 1048576 | tf_op jit(solution)/shard_map/all_to_all | solution.py:390
  76.8 12.9 %all-to-all-done.parts = bf16[8,64,512]{2,1,0:T(8,128)(2,1)S(1)} async-done(((bf16[8,64,512]{2,1,0:T(8,128)(2,1)}), bf16[8,64,512]{2,1,0:T(8,128)(2,1)S(1)}, u32[]{:S(2)}, u32[]{:S(2)}) %all-to-all-start) | async-done | bytes 524320 | tf_op jit(solution)/shard_map/all_to_all | solution.py:390
  89.8 11.1 %collective-permute-start.14 = (bf16[16,2048]{1,0:T(8,128)(2,1)S(1)}, bf16[16,2048]{1,0:T(8,128)(2,1)S(1)}, u32[]{:S(2)}, u32[]{:S(2)}) collective-permute-start(bf16[16,2048]{1,0:T(8,128)(2,1)S(1)} %get-tuple-element.35), channel_id=1, source_target_pairs={{4,0},{8,4},{12,8},{16,12},{20,16},{24,20},{28,24},{32,28},{36,32}... | collective-permute-start | bytes 196616 | tf_op jit(solution)/shard_map/ppermute | solution.py:394
  100.9 13.9 %denoise_0.1.rest_0_ = bf16[4,16,16,2048]{3,2,1,0:T(8,128)(2,1)} custom-call(s32[4]{0:T(128)S(1)} %copy-done.3, f32[4,16]{1,0:T(4,128)S(1)} %broadcast_divide_fusion.along, f32[4,16]{1,0:T(4,128)S(1)} %get-tuple-element.37.keep, f32[4,16]{1,0:T(4,128)S(1)} %get-tuple-element.36.move, bf16[4,16,16,2048]{3,2,1,0:T(8,128)(2,1)} %latent.5, ...), custom_call_target="tpu_custom_call" | custom-call | flops 2617245696 | bytes 6291456 | tf_op jit(solution)/shard_map/denoise_0/pallas_call | solution.py:317
  114.8 6.5 %denoise_3.1 = bf16[4,16,16,2048]{3,2,1,0:T(8,128)(2,1)} custom-call(s32[4]{0:T(128)S(1)} %copy-done.3, f32[4,16]{1,0:T(4,128)S(1)} %broadcast_divide_fusion.along, f32[4,16]{1,0:T(4,128)S(1)} %get-tuple-element.37.keep, f32[4,16]{1,0:T(4,128)S(1)} %get-tuple-element.36.move, bf16[4,16,16,2048]{3,2,1,0:T(8,128)(2,1)} %latent.5, ...), custom_call_target="tpu_custom_call", output_to_operand_aliasing={{}: (9, {})} | custom-call | flops 872415232 | bytes 2097152 | tf_op jit(solution)/shard_map/denoise_3/pallas_call | solution.py:317
  (45 shorter events, 5.9 us)
Async XLA Ops:
  0.6 16.0 %collective-permute-start.2 = (bf16[1024,128]{1,0:T(8,128)(2,1)}, bf16[1024,128]{1,0:T(8,128)(2,1)S(1)}, u32[]{:S(2)}, u32[]{:S(2)}) collective-permute-start(bf16[1024,128]{1,0:T(8,128)(2,1)} %param.14), channel_id=1, source_target_pairs={{0,16},{1,65},{16,32},{17,81},{32,48},{33,97},{48,0},{49,113},{64,... | collective-permute-start | bytes 786440 | tf_op jit(solution)/shard_map/ppermute | solution.py:352
  2.3 14.3 %collective-permute-start.4 = (bf16[1024,128]{1,0:T(8,128)(2,1)}, bf16[1024,128]{1,0:T(8,128)(2,1)S(1)}, u32[]{:S(2)}, u32[]{:S(2)}) collective-permute-start(bf16[1024,128]{1,0:T(8,128)(2,1)} %param.14), channel_id=1, source_target_pairs={{0,48},{1,193},{16,0},{17,209},{32,16},{33,225},{48,32},{49,241},{... | collective-permute-start | bytes 786440 | tf_op jit(solution)/shard_map/ppermute | solution.py:352
  3.9 12.7 %collective-permute-start.3 = (bf16[1024,128]{1,0:T(8,128)(2,1)}, bf16[1024,128]{1,0:T(8,128)(2,1)S(1)}, u32[]{:S(2)}, u32[]{:S(2)}) collective-permute-start(bf16[1024,128]{1,0:T(8,128)(2,1)} %param.14), channel_id=1, source_target_pairs={{0,32},{1,129},{16,48},{17,145},{32,0},{33,161},{48,16},{49,177},{... | collective-permute-start | bytes 786440 | tf_op jit(solution)/shard_map/ppermute | solution.py:352
  5.9 12.0 %collective-permute-start = (bf16[64,1024]{1,0:T(8,128)(2,1)}, bf16[64,1024]{1,0:T(8,128)(2,1)S(1)}, u32[]{:S(2)}, u32[]{:S(2)}) collective-permute-start(bf16[64,1024]{1,0:T(8,128)(2,1)} %q), channel_id=1, source_target_pairs={{0,4},{4,8},{8,12},{12,16},{16,20},{20,24},{24,28},{28,32},{32,36}... | collective-permute-start | bytes 393224 | tf_op jit(solution)/shard_map/ppermute | solution.py:371
  9.8 9.6 %collective-permute-start.1 = (bf16[64,1024]{1,0:T(8,128)(2,1)}, bf16[64,1024]{1,0:T(8,128)(2,1)S(1)}, u32[]{:S(2)}, u32[]{:S(2)}) collective-permute-start(bf16[64,1024]{1,0:T(8,128)(2,1)} %q), channel_id=1, source_target_pairs={{4,0},{8,4},{12,8},{16,12},{20,16},{24,20},{28,24},{32,28},{36,32}... | collective-permute-start | bytes 393224 | tf_op jit(solution)/shard_map/ppermute | solution.py:372
  17.7 37.0 %copy-start.4 = (bf16[4,1024,128]{2,1,0:T(8,128)(2,1)}, bf16[4,1024,128]{2,1,0:T(8,128)(2,1)S(1)}, u32[]{:S(2)}) copy-start(bf16[4,1024,128]{2,1,0:T(8,128)(2,1)S(1)} %pad_maximum_fusion.refs_4_) | copy-start | bytes 3145732
  19.4 26.3 %collective-permute-start.7 = (bf16[4,1024,128]{2,1,0:T(8,128)(2,1)S(1)}, bf16[4,1024,128]{2,1,0:T(8,128)(2,1)S(1)}, u32[]{:S(2)}, u32[]{:S(2)}) collective-permute-start(bf16[4,1024,128]{2,1,0:T(8,128)(2,1)S(1)} %pad_maximum_fusion.refs_4_), channel_id=1, source_target_pairs={{0,64},{1,17},{16,80},{17,33},{32,96},{33,49},{48,112},{49,1},{64,... | collective-permute-start | bytes 3145736 | tf_op jit(solution)/shard_map/ppermute | solution.py:352
  20.9 27.5 %collective-permute-start.12 = (bf16[4,1024,128]{2,1,0:T(8,128)(2,1)S(1)}, bf16[4,1024,128]{2,1,0:T(8,128)(2,1)}, u32[]{:S(2)}, u32[]{:S(2)}) collective-permute-start(bf16[4,1024,128]{2,1,0:T(8,128)(2,1)S(1)} %pad_maximum_fusion.refs_4_), channel_id=1, source_target_pairs={{0,192},{1,49},{16,208},{17,1},{32,224},{33,17},{48,240},{49,33},{... | collective-permute-start | bytes 3145736 | tf_op jit(solution)/shard_map/ppermute | solution.py:352
  21.4 27.0 %collective-permute-start.11 = (bf16[4,1024,128]{2,1,0:T(8,128)(2,1)S(1)}, bf16[4,1024,128]{2,1,0:T(8,128)(2,1)}, u32[]{:S(2)}, u32[]{:S(2)}) collective-permute-start(bf16[4,1024,128]{2,1,0:T(8,128)(2,1)S(1)} %pad_maximum_fusion.refs_4_), channel_id=1, source_target_pairs={{0,128},{1,33},{16,144},{17,49},{32,160},{33,1},{48,176},{49,17},{... | collective-permute-start | bytes 3145736 | tf_op jit(solution)/shard_map/ppermute | solution.py:352
  23.6 1.2 %copy-start = (bf16[2,256,1024]{2,1,0:T(8,128)(2,1)S(1)}, bf16[2,256,1024]{2,1,0:T(8,128)(2,1)}, u32[]{:S(2)}) copy-start(bf16[2,256,1024]{2,1,0:T(8,128)(2,1)} %own.3) | copy-start | bytes 3145732
  25.8 16.9 %collective-permute-start.5 = (bf16[64,1152]{1,0:T(8,128)(2,1)S(1)}, bf16[64,1152]{1,0:T(8,128)(2,1)S(1)}, u32[]{:S(2)}, u32[]{:S(2)}) collective-permute-start(bf16[64,1152]{1,0:T(8,128)(2,1)S(1)} %get-tuple-element.26), channel_id=1, source_target_pairs={{0,4},{4,8},{8,12},{12,16},{16,20},{20,24},{24,28},{28,32},{32,36}... | collective-permute-start | bytes 442376 | tf_op jit(solution)/shard_map/ppermute | solution.py:381
  27.7 15.0 %collective-permute-start.6 = (bf16[64,1152]{1,0:T(8,128)(2,1)S(1)}, bf16[64,1152]{1,0:T(8,128)(2,1)S(1)}, u32[]{:S(2)}, u32[]{:S(2)}) collective-permute-start(bf16[64,1152]{1,0:T(8,128)(2,1)S(1)} %get-tuple-element.21), channel_id=1, source_target_pairs={{4,0},{8,4},{12,8},{16,12},{20,16},{24,20},{28,24},{32,28},{36,32}... | collective-permute-start | bytes 442376 | tf_op jit(solution)/shard_map/ppermute | solution.py:380
  43.4 33.2 %copy-start.3 = (s32[4]{0:T(128)S(1)}, s32[4]{0:T(128)}, u32[]{:S(2)}) copy-start(s32[4]{0:T(128)} %count.3) | copy-start | bytes 52
  45.7 2.1 %copy-start.5 = (bf16[4,1024,128]{2,1,0:T(8,128)(2,1)}, bf16[4,1024,128]{2,1,0:T(8,128)(2,1)S(1)}, u32[]{:S(2)}) copy-start(bf16[4,1024,128]{2,1,0:T(8,128)(2,1)S(1)} %collective-permute-done.7.refs_5_) | copy-start | bytes 3145732
  45.7 7.3 %collective-permute-start.10 = (bf16[64,1024]{1,0:T(8,128)(2,1)}, bf16[64,1024]{1,0:T(8,128)(2,1)S(1)}, u32[]{:S(2)}, u32[]{:S(2)}) collective-permute-start(bf16[64,1024]{1,0:T(8,128)(2,1)} %get-tuple-element.30.refs_0_), channel_id=1, source_target_pairs={{0,12},{4,0},{8,4},{12,8},{1,13},{5,1},{9,5},{13,9},{2,14},{6,2},{... | collective-permute-start | bytes 393224 | tf_op jit(solution)/shard_map/ppermute | solution.py:386
  45.8 7.3 %collective-permute-start.9 = (bf16[64,1024]{1,0:T(8,128)(2,1)}, bf16[64,1024]{1,0:T(8,128)(2,1)S(1)}, u32[]{:S(2)}, u32[]{:S(2)}) collective-permute-start(bf16[64,1024]{1,0:T(8,128)(2,1)} %get-tuple-element.30.refs_0_), channel_id=1, source_target_pairs={{0,8},{4,12},{8,0},{12,4},{1,9},{5,13},{9,1},{13,5},{2,10},{6,14},... | collective-permute-start | bytes 393224 | tf_op jit(solution)/shard_map/ppermute | solution.py:386
  45.9 8.9 %collective-permute-start.8 = (bf16[64,1024]{1,0:T(8,128)(2,1)}, bf16[64,1024]{1,0:T(8,128)(2,1)S(1)}, u32[]{:S(2)}, u32[]{:S(2)}) collective-permute-start(bf16[64,1024]{1,0:T(8,128)(2,1)} %get-tuple-element.30.refs_0_), channel_id=1, source_target_pairs={{0,4},{4,8},{8,12},{12,0},{1,5},{5,9},{9,13},{13,1},{2,6},{6,10},{... | collective-permute-start | bytes 393224 | tf_op jit(solution)/shard_map/ppermute | solution.py:386
  48.4 52.5 %copy-start.1 = (bf16[16,128,128]{2,1,0:T(8,128)(2,1)S(1)}, bf16[16,128,128]{2,1,0:T(8,128)(2,1)}, u32[]{:S(2)}) copy-start(bf16[16,128,128]{2,1,0:T(8,128)(2,1)} %qmap.3) | copy-start | bytes 1572868
  48.4 52.5 %copy-start.2 = (bf16[16,128,128]{2,1,0:T(8,128)(2,1)S(1)}, bf16[16,128,128]{2,1,0:T(8,128)(2,1)}, u32[]{:S(2)}) copy-start(bf16[16,128,128]{2,1,0:T(8,128)(2,1)} %kmap.3) | copy-start | bytes 1572868
  53.0 1.7 %copy-start.8 = (bf16[64,1024]{1,0:T(8,128)(2,1)}, bf16[64,1024]{1,0:T(8,128)(2,1)S(1)}, u32[]{:S(2)}) copy-start(bf16[64,1024]{1,0:T(8,128)(2,1)S(1)} %collective-permute-done.10.refs_3_) | copy-start | bytes 393220
  53.0 1.7 %copy-start.9 = (bf16[64,1024]{1,0:T(8,128)(2,1)}, bf16[64,1024]{1,0:T(8,128)(2,1)S(1)}, u32[]{:S(2)}) copy-start(bf16[64,1024]{1,0:T(8,128)(2,1)S(1)} %collective-permute-done.9.refs_2_) | copy-start | bytes 393220
  62.7 2.1 %collective-permute-start.13 = (bf16[8,64,512]{2,1,0:T(8,128)(2,1)}, bf16[8,64,512]{2,1,0:T(8,128)(2,1)S(1)}, u32[]{:S(2)}, u32[]{:S(2)}) collective-permute-start(bf16[8,64,512]{2,1,0:T(8,128)(2,1)} %get-tuple-element.33), channel_id=1, source_target_pairs={{0,1},{1,0},{2,3},{3,2},{4,5},{5,4},{6,7},{7,6},{8,9},{9,8},{10,11... | collective-permute-start | bytes 1572872 | tf_op jit(solution)/shard_map/ppermute | solution.py:389
  67.0 22.7 %all-to-all-start = ((bf16[8,64,512]{2,1,0:T(8,128)(2,1)}), bf16[8,64,512]{2,1,0:T(8,128)(2,1)S(1)}, u32[]{:S(2)}, u32[]{:S(2)}) async-start(bf16[8,64,512]{2,1,0:T(8,128)(2,1)} %add_convert_fusion), calls=%async_computation | async-start | bytes 1048576 | tf_op jit(solution)/shard_map/all_to_all | solution.py:390
  89.8 25.0 %collective-permute-start.14 = (bf16[16,2048]{1,0:T(8,128)(2,1)S(1)}, bf16[16,2048]{1,0:T(8,128)(2,1)S(1)}, u32[]{:S(2)}, u32[]{:S(2)}) collective-permute-start(bf16[16,2048]{1,0:T(8,128)(2,1)S(1)} %get-tuple-element.35), channel_id=1, source_target_pairs={{4,0},{8,4},{12,8},{16,12},{20,16},{24,20},{28,24},{32,28},{36,32}... | collective-permute-start | bytes 196616 | tf_op jit(solution)/shard_map/ppermute | solution.py:394
  (3 other events, 2.0 us)
